TPU v7x, 128 devices: a whole 4x4x4 slice. The times are simulated.
128 devices in a mesh: face: 2 (over x_hi), rows: 64 (over y, z, x_lo, core).
Axes of the slice: x: 4 (x_hi: 2, x_lo: 2; x = x_hi * 2 + x_lo), y: 4, z: 4, core: 2. Of those that a mesh axis runs over, the one named last changes fastest.
Arguments:
- final_adjoint: float32 [16, 6, 1024, 1024], P(None, 'face', 'rows'), may hold values from -6 to 6
- courant_x: float32 [16, 6, 1024, 1024], P(None, 'face', 'rows'), may hold values from 0.05 to 0.45
- courant_y: float32 [16, 6, 1024, 1024], P(None, 'face', 'rows'), may hold values from 0.05 to 0.45
- ray_tiles: bfloat16 [2, 4096, 16, 512], P('face', 'rows'), may hold values from -1.5 to 1.5
- ray_innov: bfloat16 [2, 4096, 16], P('face', 'rows'), may hold values from -6 to 6
- ray_dest: int32 [2, 4096, 1], P('face', 'rows'), may hold values from 0 to 63; in each aligned block of 64 rows (0 to 63, 64 to 127, ..., all dimensions but the last counted through in order) at most 2 rows name the same one
- ray_cols: int32 [2, 4096, 32], P('face', 'rows'), may hold values from 0 to 49151
Outputs:
- prior_adjoint: float32 [16, 6, 1024, 1024], P(None, 'face', 'rows')
Inputs may be any that keep to these rules, and one draw needn't show every extreme that they name: `ray_dest`: each device's 64 ray blocks name one band each, at most 2 blocks for one band; some device sends exactly 2 blocks to some band.
All inputs are finite; a program needn't handle non-finite values.
Results may differ from a plain program's by a relative error of at most 0.0003.
Values may be sent and summed in bfloat16 or wider, within the bound.
A program may use at most 128 MiB of HBM per device.

v0:
```python
import jax
import jax.numpy as jnp
from jax import lax
from jax.sharding import PartitionSpec as P


def broadcast(value, axis, source):
    kept = jnp.where(lax.axis_index(axis) == source, value, 0).astype(value.dtype)
    return lax.psum(kept, axis)


def from_partner(block, axis, apart):
    count = lax.axis_size(axis)
    route = []
    for low in range(count):
        high = low | 1 << apart
        if high != low and high < count:
            route += [(low, high), (high, low)]
    return lax.ppermute(block, axis, route)


def shifted(value, axis, by):
    count = lax.axis_size(axis)
    return lax.ppermute(value, axis, [(i, (i + by) % count) for i in range(count)])


def spread(payload, band_id, band):
    whole_edge = broadcast(payload.astype(jnp.bfloat16), "rows", 0).astype(payload.dtype)
    return lax.dynamic_slice_in_dim(whole_edge, band_id * band, band, 2)


def trade(packet):
    return from_partner(packet.astype(jnp.bfloat16), "face", 0).astype(packet.dtype)


def transpose_step(adjoint, courant_x, courant_y):
    levels, faces, band, edge = adjoint.shape
    bands = lax.axis_size("rows")
    band_id = lax.axis_index("rows")
    first = lax.axis_index("face") == 0
    along = courant_x * adjoint
    upward = courant_y * adjoint
    result = (1.0 - courant_x - courant_y) * adjoint
    result = result + jnp.pad(along[..., 1:], ((0, 0), (0, 0), (0, 0), (0, 1)))
    result = result + jnp.pad(upward[:, :, 1:, :], ((0, 0), (0, 0), (0, 1), (0, 0)))
    side = along[..., 0]
    top_row = upward[:, :, 0, :]
    below = shifted(top_row, "rows", -1)
    zero_row = jnp.zeros_like(below[:, 0])
    seam_local = jnp.where(
        first,
        jnp.stack([zero_row, zero_row, below[:, 1]], axis=1),
        jnp.stack([zero_row, below[:, 0], zero_row], axis=1),
    )
    mirrored = top_row[..., ::-1]
    out_rot = jnp.where(first, mirrored[:, 2], mirrored[:, 1])
    loc_rot = jnp.where(first, mirrored[:, 0], zero_row)
    received = trade(jnp.concatenate([out_rot, side[:, 0], below[:, 2]], axis=-1))
    far_side = received[:, edge : edge + band]
    far_unrot = received[:, edge + band :]
    piece = spread(jnp.stack([received[:, :edge], loc_rot], axis=1), band_id, band)
    cross = piece[:, 0]
    local = piece[:, 1]
    zero_piece = jnp.zeros_like(cross)
    col_add = jnp.stack(
        [jnp.where(first, cross, zero_piece), jnp.where(first, zero_piece, cross), local], axis=1
    )
    zero_unrot = jnp.zeros_like(far_unrot)
    cross_unrot = jnp.stack(
        [jnp.where(first, far_unrot, zero_unrot), zero_unrot, zero_unrot], axis=1
    )
    bottom = jnp.where(band_id == bands - 1, seam_local + cross_unrot, below)
    right_col = jnp.concatenate([side[:, 1:, :], far_side[:, None, :]], axis=1)
    result = result.at[:, :, band - 1, :].add(bottom)
    result = result.at[:, :, :, 0].add(col_add)
    result = result.at[:, :, :, edge - 1].add(right_col)
    return result


def ray_forcing(ray_tiles, ray_innov, ray_dest, ray_cols, field_shape):
    tiles = ray_tiles[0]
    innov = ray_innov[0]
    target = ray_dest[0][:, 0]
    cells = ray_cols[0]
    bands = lax.axis_size("rows")
    blocks = tiles.shape[0]
    slots = max(2, 2 * blocks // bands)
    hits = (target[:, None] == jnp.arange(bands, dtype=jnp.int32)[None, :]).astype(jnp.int32)
    order = jnp.sum(jnp.cumsum(hits, axis=0) * hits, axis=1) - 1
    slot_id = target * slots + order
    cell_buf = jnp.zeros((bands * slots, cells.shape[1]), jnp.int32).at[slot_id].set(cells)
    cell_buf = cell_buf.reshape(bands, slots, cells.shape[1])
    cell_got = lax.all_to_all(cell_buf, "rows", split_axis=0, concat_axis=0, tiled=True)
    contrib = jnp.einsum("br,brk->bk", innov, tiles, preferred_element_type=jnp.float32)
    sum_buf = jnp.zeros((bands * slots, contrib.shape[1]), jnp.float32).at[slot_id].set(contrib)
    sum_buf = sum_buf.reshape(bands, slots, contrib.shape[1])
    sums = lax.all_to_all(sum_buf, "rows", split_axis=0, concat_axis=0, tiled=True)
    levels = field_shape[0]
    width = cell_got.shape[2]
    values = jnp.transpose(sums.reshape(-1, levels, width), (1, 0, 2)).reshape(levels, -1)
    total = field_shape[1] * field_shape[2] * field_shape[3]
    flat = jnp.zeros((levels, total), jnp.float32).at[:, cell_got.reshape(-1)].add(values)
    return flat.reshape(field_shape)


def per_device(final_adjoint, courant_x, courant_y, ray_tiles, ray_innov, ray_dest, ray_cols):
    forcing = ray_forcing(ray_tiles, ray_innov, ray_dest, ray_cols, final_adjoint.shape)
    mid_adjoint = transpose_step(final_adjoint, courant_x, courant_y) + forcing
    return transpose_step(mid_adjoint, courant_x, courant_y)


def solution(mesh):
    placed = (
        P(None, "face", "rows", None),
        P(None, "face", "rows", None),
        P(None, "face", "rows", None),
        P("face", "rows", None, None),
        P("face", "rows", None),
        P("face", "rows", None),
        P("face", "rows", None),
    )
    return jax.shard_map(
        per_device,
        mesh=mesh,
        in_specs=placed,
        out_specs=P(None, "face", "rows", None),
        check_vma=False,
    )
```

profile of v0, /device:TPU:0, one launch (start us, length us, event | category | flops | bytes accessed | tf_op | source)
XLA Modules:
  0.0 1121.3 jit_solution(1010042079518016696)
XLA Ops:
  11.1 10.0 all-to-all-start
  21.0 4.8 fusion.28
  26.0 5.9 collective-permute-start
  32.0 2.2 slice.335
  34.2 2.5 slice.334
  40.1 9.5 pad_add_fusion.1
  52.0 4.6 all-to-all-start.1
  58.1 2.7 collective-permute-start.1
  60.9 5.7 all-to-all-done.1
  68.5 34.9 %scatter_custom_fusion.2 = f32[16,49152]{0,1:T(8,128)} fusion(s32[4096]{0:T(1024)} %bitcast.82, f32[4096,16]{1,0:T(8,128)S(1)} %copy.228, f32[]{:T(128)} %constant.172.clone.1), kind=kCustom, calls=%fused_computation.3 | custom fusion | flops 65536 | bytes 3146240 | tf_op jit(solution)/shard_map/scatter-add | solution.py:102
  103.4 16.0 %copy.237 = f32[16,3,16,1024]{3,2,1,0:T(8,128)} copy(f32[16,3,16,1024]{0,3,2,1:T(8,128)} %bitcast.70) | data formatting | bytes 6291456 | tf_op jit(solution)/shard_map/reshape | solution.py:103
  122.5 4.8 scatter-add.26
  127.3 463.0 %all-reduce.11.cloned.1.call-done = bf16[16,2,1024]{2,0,1:T(8,128)(2,1)} async-done(((bf16[16,2,1024]{2,0,1:T(8,128)(2,1)}), bf16[16,2,1024]{2,0,1:T(8,128)(2,1)}) %all-reduce.11.cloned.1.call-update) | async-done | bytes 65552 | tf_op jit(solution)/shard_map/psum | solution.py:9
  592.5 2.3 scatter-add.29
  596.0 5.6 scatter-add.30
  601.6 6.1 add_multiply_fusion.1
  611.8 2.6 slice.354
  616.7 10.8 pad_add_fusion
  627.6 2.8 collective-permute-start.3
  630.4 3.1 collective-permute-done.3
  636.2 4.8 scatter-add.34
  641.3 461.9 %all-reduce.13.cloned.1.call-done = bf16[16,2,1024]{2,0,1:T(8,128)(2,1)} async-done(((bf16[16,2,1024]{2,0,1:T(8,128)(2,1)}), bf16[16,2,1024]{2,0,1:T(8,128)(2,1)}) %all-reduce.13.cloned.1.call-update) | async-done | bytes 65552 | tf_op jit(solution)/shard_map/psum | solution.py:9
  1105.4 2.3 scatter-add.42
  1108.9 5.5 scatter-add.43
  (97 shorter events, 32.9 us)
Async XLA Ops:
  6.5 32.6 %copy-start = (bf16[1,64,16,512]{3,2,1,0:T(8,128)(2,1)S(1)}, bf16[1,64,16,512]{3,2,1,0:T(8,128)(2,1)}, u32[]{:S(2)}) copy-start(bf16[1,64,16,512]{3,2,1,0:T(8,128)(2,1)} %param.22) | copy-start | bytes 3145732
  11.1 40.9 %all-to-all-start = ((s32[64,2,32]{2,1,0:T(2,128)}), s32[64,2,32]{2,1,0:T(2,128)S(1)}, u32[]{:S(2)}, u32[]{:S(2)}) async-start(s32[64,2,32]{2,1,0:T(2,128)} %bitcast.16), calls=%async_computation | async-start | bytes 131072 | tf_op jit(solution)/shard_map/all_to_all | solution.py:93
  26.0 31.3 %collective-permute-start = (f32[16,3,1024]{2,0,1:T(8,128)S(1)}, f32[16,3,1024]{2,0,1:T(8,128)S(1)}, u32[]{:S(2)}, u32[]{:S(2)}) collective-permute-start(f32[16,3,1024]{2,0,1:T(8,128)S(1)} %bitcast.73), channel_id=1, source_target_pairs={{0,63},{1,0},{2,1},{3,2},{4,3},{5,4},{6,5},{7,6},{8,7},{9,8},{10,9... | collective-permute-start | bytes 589832 | tf_op jit(solution)/shard_map/ppermute | solution.py:24
  34.2 2.5 copy-start.4
  52.0 14.6 %all-to-all-start.1 = ((f32[64,2,512]{2,1,0:T(2,128)}), f32[64,2,512]{2,1,0:T(2,128)S(1)}, u32[]{:S(2)}, u32[]{:S(2)}) async-start(f32[64,2,512]{2,1,0:T(2,128)} %reshape.299), calls=%async_computation.1 | async-start | bytes 524288 | tf_op jit(solution)/shard_map/all_to_all | solution.py:97
  56.6 533.7 %all-reduce.11.cloned.1.call-start = ((), (), s32[]{:S(2)}) async-start(), calls=%async_computation.2 | async-start | bytes 131072 | tf_op jit(solution)/shard_map/psum | solution.py:9
  58.1 61.3 %collective-permute-start.1 = (bf16[16,2064]{1,0:T(8,128)(2,1)}, bf16[16,2064]{1,0:T(8,128)(2,1)S(1)}, u32[]{:S(2)}, u32[]{:S(2)}) collective-permute-start(bf16[16,2064]{1,0:T(8,128)(2,1)} %concatenate.26), channel_id=1, source_target_pairs={{0,64},{64,0},{1,65},{65,1},{2,66},{66,2},{3,67},{67,3},{4,68},{68... | collective-permute-start | bytes 198152 | tf_op jit(solution)/shard_map/ppermute | solution.py:19
  103.4 16.1 %copy-start.2 = (bf16[16,1,1024]{2,0,1:T(8,128)(2,1)S(1)}, bf16[16,1,1024]{2,0,1:T(8,128)(2,1)}, u32[]{:S(2)}) copy-start(bf16[16,1,1024]{2,0,1:T(8,128)(2,1)} %select_convert_fusion.2) | copy-start | bytes 98308
  103.4 18.7 %copy-start.3 = (f32[16,2,16]{2,0,1:T(8,128)S(1)}, f32[16,2,16]{2,0,1:T(8,128)}, u32[]{:S(2)}) copy-start(f32[16,2,16]{2,0,1:T(8,128)} %slice.352) | copy-start | bytes 6148
  120.2 983.0 %all-reduce.13.cloned.1.call-start = ((), (), s32[]{:S(2)}) async-start(), calls=%async_computation.3 | async-start | bytes 131072 | tf_op jit(solution)/shard_map/psum | solution.py:9
  610.1 17.4 %collective-permute-start.2 = (f32[16,3,1024]{2,0,1:T(8,128)S(1)}, f32[16,3,1024]{2,0,1:T(8,128)S(1)}, u32[]{:S(2)}, u32[]{:S(2)}) collective-permute-start(f32[16,3,1024]{2,0,1:T(8,128)S(1)} %bitcast.76), channel_id=1, source_target_pairs={{0,63},{1,0},{2,1},{3,2},{4,3},{5,4},{6,5},{7,6},{8,7},{9,8},{10,9... | collective-permute-start | bytes 589832 | tf_op jit(solution)/shard_map/ppermute | solution.py:24
  627.6 5.9 collective-permute-start.3
  634.3 480.2 %copy-start.1 = (bf16[1,64,16,512]{3,2,1,0:T(8,128)(2,1)S(1)}, bf16[1,64,16,512]{3,2,1,0:T(8,128)(2,1)}, u32[]{:S(2)}) copy-start(bf16[1,64,16,512]{3,2,1,0:T(8,128)(2,1)} %param.22) | copy-start | bytes 3145732
Sparse Core Ops, SparseCore 0:
  120.4 469.9 all-reduce.10
  634.4 468.7 all-reduce.12
where the time goes:
time: 1120 us
  waiting for transfers between devices  934 us (83%)
  other arithmetic  81 us (7%)
  local copies, waits for them, and re-layouts  64.7 us (6%)
  starting transfers between devices  27.7 us (2%)
  between operations  13.7 us (1%)
    psum x2, waiting for transfers between devices, broadcast(): return lax.psum(kept, axis)  925 us
    scatter-add x1, other arithmetic, ray_forcing(): jnp.zeros((levels, total), jnp.float32).at[:, cell_got.reshape(-1)]  34.9 us
  transfers between devices with their start and end apart: 8, of which 4 were waited for; matrix products, arithmetic and copies ran while one was open for 10% of the time, Pallas kernels for 0%

commit v1 on v0

v1 whole, which is shorter than its diff:
```python
import functools

import jax
import jax.numpy as jnp
from jax import lax
from jax.experimental import pallas as pl
from jax.experimental.pallas import tpu as pltpu
from jax.sharding import PartitionSpec as P

LEV, LF, RD, NC = 16, 3, 16, 1024
BANDS, RAYS, K, CAP = 64, 16, 32, 2
GROUP = 8
RELAYS = BANDS // GROUP
LANES = 128
PACK = 16
SENT = 9
COPIES = 4
F32, BF16, I32 = jnp.float32, jnp.bfloat16, jnp.int32
MESH = pl.DeviceIdType.MESH


def iota(shape, dim):
    return lax.broadcasted_iota(I32, shape, dim)


def dot(a, b):
    return jnp.dot(a, b, preferred_element_type=F32)


class Halo:
    def __init__(self, tops, sides, below, side_in, rot, sems):
        self.tops, self.sides, self.below, self.side_in, self.rot = tops, sides, below, side_in, rot
        self.send, self.recv, self.rot_send, self.fwd_send, self.rot_recv = sems
        self.g = lax.axis_index("face")
        self.b = lax.axis_index("rows")

    def greet(self, barrier):
        g, b = self.g, self.b

        def hello(face, band):
            pl.semaphore_signal(barrier, inc=1, device_id=(face, band), device_id_type=MESH)

        hello(1 - g, b)

        @pl.when(b < BANDS - 1)
        def _():
            hello(g, b + 1)

        @pl.when(b == BANDS - 1)
        def _():
            hello(g, 0)

        @pl.when((b == BANDS - 1) & (g == 0))
        def _():
            hello(1, 0)

        @pl.when(b % GROUP != 0)
        def _():
            hello(g, b // GROUP * GROUP)

        @pl.when(b % GROUP == 0)
        def _():
            hello(1 - g, 0)

        @pl.when((b % GROUP == 0) & (g == 0) & (b != 0))
        def _():
            hello(0, 0)

        relay = (b % GROUP == 0).astype(I32)
        origin = (b == 0).astype(I32)
        return 2 + relay * (GROUP - 1) + origin * (RELAYS + jnp.where(g == 0, RELAYS - 1, 1))

    def zero(self):
        g, b = self.g, self.b
        edge = jnp.zeros((LEV, NC), F32)

        @pl.when(b == BANDS - 1)
        def _():
            @pl.when(g == 0)
            def _():
                self.below[1] = edge

            @pl.when(g == 1)
            def _():
                self.below[0] = edge
                self.below[2] = edge

        @pl.when(g == 1)
        def _():
            self.rot[1] = jnp.zeros((LEV, LANES), F32)

    def copy(self, src, dst, send, recv, face, band):
        return pltpu.make_async_remote_copy(
            src_ref=src, dst_ref=dst, send_sem=send, recv_sem=recv,
            device_id=(face, band), device_id_type=MESH,
        )

    def row(self, face):
        return self.copy(self.tops, self.below, self.send.at[0], self.recv.at[0], self.g, face)

    def one(self, src, dst, face, slot):
        return self.copy(
            self.tops.at[src], self.below.at[dst], self.send.at[slot], self.recv.at[slot], face, BANDS - 1
        )

    def side(self):
        return self.copy(self.sides, self.side_in, self.send.at[1], self.recv.at[1], 1 - self.g, self.b)

    def piece(self, src, dst, face, r, n):
        lanes = pl.ds(LANES * (RELAYS - 1 - r), LANES)
        return self.copy(
            self.tops.at[src, :, lanes], self.rot.at[dst], self.rot_send.at[dst, r], self.rot_recv.at[dst],
            face, n,
        )

    def start(self):
        g, b = self.g, self.b

        @pl.when(b == 0)
        def _():
            @pl.when(g == 0)
            def _():
                for r in range(RELAYS):
                    self.piece(2, 0, 1, r, r * GROUP).start()
                for r in range(1, RELAYS):
                    self.piece(0, 1, 0, r, r * GROUP).start()
                self.one(1, 2, 0, 0).start()
                self.rot[1] = self.tops[0, :, NC - LANES :]

            @pl.when(g == 1)
            def _():
                for r in range(RELAYS):
                    self.piece(1, 0, 0, r, r * GROUP).start()
                self.one(0, 1, 1, 0).start()
                self.one(2, 0, 0, 2).start()

        @pl.when(b != 0)
        def _():
            self.row(b - 1).start()

        self.side().start()

    def forward(self, dst, i):
        return self.copy(
            self.rot.at[dst], self.rot.at[dst], self.fwd_send.at[dst, i], self.rot_recv.at[dst],
            self.g, self.b // GROUP * GROUP + i,
        )

    def relay(self):
        g, b = self.g, self.b

        @pl.when(b % GROUP == 0)
        def _():
            self.forward(0, 1).wait_recv()
            for i in range(1, GROUP):
                self.forward(0, i).start()

            @pl.when(g == 0)
            def _():
                @pl.when(b != 0)
                def _():
                    self.forward(1, 1).wait_recv()

                for i in range(1, GROUP):
                    self.forward(1, i).start()

    def wait(self):
        g, b = self.g, self.b

        @pl.when(b % GROUP != 0)
        def _():
            self.forward(0, 1).wait_recv()

            @pl.when(g == 0)
            def _():
                self.forward(1, 1).wait_recv()

        self.side().wait_recv()

        @pl.when(b != BANDS - 1)
        def _():
            self.row(0).wait_recv()

        @pl.when(b == BANDS - 1)
        def _():
            @pl.when(g == 0)
            def _():
                self.one(1, 2, 0, 0).wait_recv()
                self.one(2, 0, 0, 2).wait_recv()

            @pl.when(g == 1)
            def _():
                self.one(0, 1, 1, 0).wait_recv()

    def finish(self):
        g, b = self.g, self.b
        self.side().wait_send()

        @pl.when(b != 0)
        def _():
            self.row(0).wait_send()

        @pl.when(b == 0)
        def _():
            @pl.when(g == 0)
            def _():
                for r in range(RELAYS):
                    self.piece(2, 0, 1, r, r * GROUP).wait_send()
                for r in range(1, RELAYS):
                    self.piece(0, 1, 0, r, r * GROUP).wait_send()
                self.one(1, 2, 0, 0).wait_send()

            @pl.when(g == 1)
            def _():
                for r in range(RELAYS):
                    self.piece(1, 0, 0, r, r * GROUP).wait_send()
                self.one(0, 1, 1, 0).wait_send()
                self.one(2, 0, 0, 2).wait_send()

        @pl.when(b % GROUP == 0)
        def _():
            for i in range(1, GROUP):
                self.forward(0, i).wait_send()

            @pl.when(g == 0)
            def _():
                for i in range(1, GROUP):
                    self.forward(1, i).wait_send()


def halo_scratch():
    return [
        pltpu.VMEM((LF, LEV, NC), F32),
        pltpu.VMEM((RD, LANES), F32),
        pltpu.VMEM((LF, LEV, NC), F32),
        pltpu.VMEM((RD, LANES), F32),
        pltpu.VMEM((2, LEV, LANES), F32),
        pltpu.SemaphoreType.DMA((3,)),
        pltpu.SemaphoreType.DMA((3,)),
        pltpu.SemaphoreType.DMA((2, RELAYS)),
        pltpu.SemaphoreType.DMA((2, GROUP)),
        pltpu.SemaphoreType.DMA((2,)),
    ]


def edges(a, cx, cy, tops, sides):
    lane = iota((RD, LANES), 1)

    def body(l, acc):
        for f in range(LF):
            tops[f, pl.ds(l, 1), :] = cy[l, f, 0:1, :] * a[l, f, 0:1, :]
        along = cx[l, 0, :, 0:LANES] * a[l, 0, :, 0:LANES]
        return jnp.where(lane == l, jnp.broadcast_to(along[:, 0:1], (RD, LANES)), acc)

    sides[...] = lax.fori_loop(0, LEV, body, jnp.zeros((RD, LANES), F32))


def interior(a, cx, cy, out, lo, hi):
    row = iota((RD, NC), 0)
    col = iota((RD, NC), 1)

    def body(l, carry):
        base, rolled = [], []
        for f in range(LF):
            value, x, y = a[l, f], cx[l, f], cy[l, f]
            along, upward = x * value, y * value
            rolled.append(pltpu.roll(along, NC - 1, 1))
            lifted = jnp.where(row < RD - 1, pltpu.roll(upward, RD - 1, 0), 0.0)
            base.append((1.0 - x - y) * value + lifted)
        for f in range(LF):
            beyond = rolled[f + 1] if f + 1 < LF else 0.0
            out[l, f] = base[f] + jnp.where(col < NC - 1, rolled[f], beyond)
        return carry

    lax.fori_loop(lo, hi, body, 0)


def patch(out, below, side_in, rot):
    g = lax.axis_index("face")
    b = lax.axis_index("rows")
    row = iota((8, NC), 0)
    lane = iota((RD, LANES), 1)
    place = LANES - 1 - RD * (b % GROUP) - iota((RD, LANES), 0)

    def body(l, carry):
        for f in range(LF):
            edge = jnp.broadcast_to(below[f, pl.ds(l, 1), :], (8, NC))
            out[l, f, 8:RD, :] += jnp.where(row == 7, edge, 0.0)

        def column(piece):
            picked = jnp.where(lane == place, jnp.broadcast_to(piece, (RD, LANES)), 0.0)
            return jnp.where(lane == 0, jnp.sum(picked, axis=1, keepdims=True), 0.0)

        cross = column(rot[0, pl.ds(l, 1), :])
        local = column(rot[1, pl.ds(l, 1), :])
        right = jnp.sum(jnp.where(lane == l, side_in[...], 0.0), axis=1, keepdims=True)
        out[l, 0, :, 0:LANES] += jnp.where(g == 0, cross, 0.0)
        out[l, 1, :, 0:LANES] += jnp.where(g == 1, cross, 0.0)
        out[l, 2, :, 0:LANES] += local
        out[l, 2, :, NC - LANES :] += jnp.where(lane == LANES - 1, right, 0.0)
        return carry

    lax.fori_loop(0, LEV, body, 0)


def pack(tiles, innov, dest, cells, send):
    blocks = BANDS
    wide = blocks * RAYS
    spread = (iota((RAYS, wide), 1) % RAYS == iota((RAYS, wide), 0)).astype(BF16)
    own = iota((blocks, wide), 1) // RAYS == iota((blocks, wide), 0)
    diag = jnp.where(own, dot(innov[0], spread), 0.0).astype(BF16)

    target = jnp.broadcast_to(dest[0], (blocks, blocks))
    before, after = iota((blocks, blocks), 0), iota((blocks, blocks), 1)
    targets = jnp.sum(jnp.where(before == after, target, 0).astype(F32), axis=0, keepdims=True)
    same = (target.astype(F32) == targets) & (before < after)
    orders = jnp.sum(same.astype(F32), axis=0, keepdims=True)
    slot = iota((CAP * BANDS, blocks), 0)
    chosen = ((slot % BANDS).astype(F32) == targets) & ((slot // BANDS).astype(F32) == orders)
    chosen = chosen.astype(BF16)

    src, dst = iota((LEV * K, LEV * K), 0), iota((LEV * K, LEV * K), 1)
    level, part, inner = dst % LANES // 8, dst // LANES, dst % 8
    mixed = (src == level * K + part * 8 + inner).astype(BF16)
    weights = dot(tiles[0].reshape(wide, LEV * K), mixed).astype(BF16)
    sums = dot(dot(chosen, diag).astype(BF16), weights)

    cell = cells[0]
    code = ((cell // (8 * NC)) * NC + cell % NC) * 8 + cell // NC % 8
    high, low = (code // 256).astype(F32).astype(BF16), (code % 256).astype(F32).astype(BF16)
    codes = dot(chosen, high) * 256.0 + dot(chosen, low)
    codes = jnp.concatenate(
        [codes[:BANDS], codes[BANDS:], jnp.zeros((BANDS, LANES - 2 * K), F32)], axis=1
    )
    flat = send.reshape(BANDS * PACK, LANES)
    for s in range(CAP):
        for q in range(4):
            flat[pl.ds(s * 4 + q, BANDS, stride=PACK), :] = sums[
                s * BANDS : (s + 1) * BANDS, q * LANES : (q + 1) * LANES
            ]
    flat[pl.ds(SENT - 1, BANDS, stride=PACK), :] = codes


def first_kernel(
    a_hbm, cx_hbm, cy_hbm, tiles, innov, dest, cells, out, recv,
    a, cx, cy, send, load_sem, pack_send, pack_recv, own_sem, tops, sides, below, side_in, rot, *sems,
):
    g = lax.axis_index("face")
    b = lax.axis_index("rows")
    loads = [
        pltpu.make_async_copy(src, dst, load_sem.at[i])
        for i, (src, dst) in enumerate(((a_hbm, a), (cy_hbm, cy), (cx_hbm, cx)))
    ]
    for load in loads:
        load.start()
    halo = Halo(tops, sides, below, side_in, rot, sems)
    barrier = pltpu.get_barrier_semaphore()
    expected = halo.greet(barrier) + BANDS - 1

    def hello(i, carry):
        pl.semaphore_signal(barrier, inc=1, device_id=(g, (b + i) % BANDS), device_id_type=MESH)
        return carry

    lax.fori_loop(1, BANDS, hello, 0)
    halo.zero()
    pack(tiles, innov, dest, cells, send)
    pl.semaphore_wait(barrier, expected)

    def packet(band):
        return pltpu.make_async_remote_copy(
            src_ref=send.at[band, pl.ds(0, SENT)],
            dst_ref=recv.at[b, pl.ds(0, SENT)],
            send_sem=pack_send,
            recv_sem=pack_recv.at[b],
            device_id=(g, band),
            device_id_type=MESH,
        )

    def ship(i, carry):
        packet((b + i) % BANDS).start()
        return carry

    lax.fori_loop(1, BANDS, ship, 0)
    own = pltpu.make_async_copy(send.at[b, pl.ds(0, SENT)], recv.at[b, pl.ds(0, SENT)], own_sem)
    own.start()
    for load in loads:
        load.wait()
    edges(a, cx, cy, tops, sides)
    halo.start()
    interior(a, cx, cy, out, 0, LEV // 2)
    halo.relay()
    interior(a, cx, cy, out, LEV // 2, LEV)
    halo.wait()
    patch(out, below, side_in, rot)
    halo.finish()
    own.wait()

    def landed(i, carry):
        band = (b + i) % BANDS
        pltpu.make_async_remote_copy(
            src_ref=send.at[band, pl.ds(0, SENT)],
            dst_ref=recv.at[band, pl.ds(0, SENT)],
            send_sem=pack_send,
            recv_sem=pack_recv.at[band],
            device_id=(g, band),
            device_id_type=MESH,
        ).wait()
        return carry

    lax.fori_loop(1, BANDS, landed, 0)


def scatter_kernel(recv, dense_hbm, out, dense, index, index_s, values, *rest):
    fields, (load_sem, index_sem) = rest[:COPIES], rest[COPIES:]
    load = pltpu.make_async_copy(dense_hbm, dense, load_sem)
    load.start()
    flat = recv.reshape(BANDS * PACK, LANES)
    index[...] = flat[pl.ds(SENT - 1, BANDS, stride=PACK), :].astype(I32)
    to_scalar = pltpu.make_async_copy(index, index_s, index_sem)
    to_scalar.start()

    step = 8
    rows = step * CAP * 4
    inner = iota((rows, 8, LANES), 2) % 8 == iota((rows, 8, LANES), 1)
    widen = (iota((LANES, LANES), 0) // 8 == iota((LANES, LANES), 1) // 8).astype(BF16)

    def expand(i, carry):
        got = recv[pl.ds(i * step, step), 0 : CAP * 4, :].reshape(rows, 1, LANES)
        one = jnp.where(inner, jnp.broadcast_to(got, (rows, 8, LANES)), 0.0).reshape(rows * 8, LANES)
        high = one.astype(BF16)
        rest = one - high.astype(F32)
        mid = rest.astype(BF16)
        low = (rest - mid.astype(F32)).astype(BF16)
        values[pl.ds(i * rows * 8, rows * 8), :] = dot(high, widen) + dot(mid, widen) + dot(low, widen)
        return carry

    lax.fori_loop(0, BANDS // step, expand, 0)

    def clear(i, carry):
        for field in fields:
            field[pl.ds(i * LANES, LANES), :] = jnp.zeros((LANES, LANES), F32)
        return carry

    lax.fori_loop(0, LF * 2 * NC // LANES, clear, 0)
    to_scalar.wait()
    lane = iota((1, LANES), 1) % 8
    entries = CAP * K

    def add(i, carry):
        for e in range(entries):
            code = index_s[i, e]
            line = values[pl.ds(i * entries + e, 1), :]
            field = fields[e % COPIES]
            field[pl.ds(code // 8, 1), :] += jnp.where(lane == code % 8, line, 0.0)
        return carry

    lax.fori_loop(0, BANDS, add, 0)
    load.wait()

    def turn(i, carry):
        f, half = i // 2, i % 2
        for c in range(NC // LANES):
            block = sum(field[pl.ds(i * NC + c * LANES, LANES), :] for field in fields)
            turned = block.T.reshape(LEV, 8, LANES)
            rows = pl.ds(pl.multiple_of(half * 8, 8), 8)
            cols = pl.ds(c * LANES, LANES)
            out[:, f, rows, cols] = dense[:, f, rows, cols] + turned
        return carry

    lax.fori_loop(0, LF * 2, turn, 0)


def last_kernel(
    a_hbm, cx_hbm, cy_hbm, out, a, cx, cy, load_sem, tops, sides, below, side_in, rot, *sems
):
    loads = [
        pltpu.make_async_copy(src, dst, load_sem.at[i])
        for i, (src, dst) in enumerate(((a_hbm, a), (cy_hbm, cy), (cx_hbm, cx)))
    ]
    for load in loads:
        load.start()
    halo = Halo(tops, sides, below, side_in, rot, sems)
    barrier = pltpu.get_barrier_semaphore()
    expected = halo.greet(barrier)
    halo.zero()
    for load in loads:
        load.wait()
    edges(a, cx, cy, tops, sides)
    pl.semaphore_wait(barrier, expected)
    halo.start()
    interior(a, cx, cy, out, 0, LEV // 2)
    halo.relay()
    interior(a, cx, cy, out, LEV // 2, LEV)
    halo.wait()
    patch(out, below, side_in, rot)
    halo.finish()


FIELD = (LEV, LF, RD, NC)


def params(cid=None):
    kw = {} if cid is None else dict(collective_id=cid, has_side_effects=True)
    return pltpu.CompilerParams(vmem_limit_bytes=48 * 1024 * 1024, **kw)


def per_device(final_adjoint, courant_x, courant_y, ray_tiles, ray_innov, ray_dest, ray_cols):
    vmem, anywhere = pl.BlockSpec(memory_space=pltpu.VMEM), pl.BlockSpec(memory_space=pl.ANY)
    field = jax.ShapeDtypeStruct(FIELD, F32)
    held = pltpu.VMEM(FIELD, F32)
    dense, recv = pl.pallas_call(
        first_kernel,
        out_shape=(field, jax.ShapeDtypeStruct((BANDS, PACK, LANES), F32)),
        in_specs=[anywhere] * 3 + [vmem] * 4,
        out_specs=(vmem, anywhere),
        scratch_shapes=[
            held, held, held,
            pltpu.VMEM((BANDS, PACK, LANES), F32),
            pltpu.SemaphoreType.DMA((3,)),
            pltpu.SemaphoreType.DMA,
            pltpu.SemaphoreType.DMA((BANDS,)),
            pltpu.SemaphoreType.DMA,
        ] + halo_scratch(),
        compiler_params=params(0),
        name="sums_and_first_step",
    )(final_adjoint, courant_x, courant_y, ray_tiles, ray_innov, ray_dest, ray_cols)
    mid = pl.pallas_call(
        scatter_kernel,
        out_shape=field,
        in_specs=[vmem, anywhere],
        out_specs=vmem,
        scratch_shapes=[
            held,
            pltpu.VMEM((BANDS, LANES), I32),
            pltpu.SMEM((BANDS, LANES), I32),
            pltpu.VMEM((BANDS * CAP * K, LANES), F32),
        ] + [pltpu.VMEM((LF * 2 * NC, LANES), F32)] * COPIES + [
            pltpu.SemaphoreType.DMA,
            pltpu.SemaphoreType.DMA,
        ],
        compiler_params=params(),
        name="forcing",
    )(recv, dense)
    return pl.pallas_call(
        last_kernel,
        out_shape=field,
        in_specs=[anywhere] * 3,
        out_specs=vmem,
        scratch_shapes=[held, held, held, pltpu.SemaphoreType.DMA((3,))] + halo_scratch(),
        compiler_params=params(1),
        name="second_step",
    )(mid, courant_x, courant_y)


def solution(mesh):
    placed = (
        P(None, "face", "rows", None),
        P(None, "face", "rows", None),
        P(None, "face", "rows", None),
        P("face", "rows", None, None),
        P("face", "rows", None),
        P("face", "rows", None),
        P("face", "rows", None),
    )
    return jax.shard_map(
        per_device,
        mesh=mesh,
        in_specs=placed,
        out_specs=P(None, "face", "rows", None),
        check_vma=False,
    )
```

time: 1120 us -> 72.5 us (0.06)
  the two profiles are of different devices: /device:TPU:0 before, /device:TPU:27 now
where the time goes in v1:
time: 72.5 us; the launch traced here: 72.3 us
  Pallas kernels  63.7 us (88%)
  local copies, waits for them, and re-layouts  8.53 us (12%)
    pallas_call x1, Pallas kernels, per_device(): pl.pallas_call(scatter_kernel, out_shape=field, in_specs=[vmem, anywhere]...  28.3 us
    pallas_call x1, Pallas kernels, per_device(): pl.pallas_call(first_kernel, out_shape=(field, jax.ShapeDtypeStruct((BAND...  21 us
    pallas_call x1, Pallas kernels, per_device(): pl.pallas_call(last_kernel, out_shape=field, in_specs=[anywhere] * 3, out...  14.4 us
    unnamed x10, local copies, waits for them, and re-layouts  8.53 us

profile of v1, /device:TPU:27, one launch (start us, length us, event | category | flops | bytes accessed | tf_op | source)
XLA Modules:
  0.0 72.3 jit_solution(15440693561056037136)
XLA Ops:
  0.0 0.8 %copy.8.innov = bf16[1,64,16]{2,1,0:T(8,128)(2,1)S(1)} copy(bf16[1,64,16]{1,2,0:T(8,128)(2,1)} %param.11) | data formatting | bytes 4096 | tf_op args[4]
  0.8 0.7 %copy.9.dest = s32[1,64,1]{2,1,0:T(8,128)S(1)} copy(s32[1,64,1]{1,2,0:T(1,128)} %param.12) | data formatting | bytes 512 | tf_op args[5]
  1.5 0.8 %copy.10.cells = s32[1,64,32]{2,1,0:T(8,128)S(1)} copy(s32[1,64,32]{1,2,0:T(8,128)} %param.13) | data formatting | bytes 16384 | tf_op args[6]
  2.3 0.0 copy-start.2
  2.3 1.2 %copy-done.2 = bf16[1,64,16,512]{3,2,1,0:T(8,128)(2,1)S(1)} copy-done((bf16[1,64,16,512]{3,2,1,0:T(8,128)(2,1)S(1)}, bf16[1,64,16,512]{3,2,1,0:T(8,128)(2,1)}, u32[]{:S(2)}) %copy-start.2) | copy-done | bytes 1048600
  3.6 21.0 %sums_and_first_step.1 = (f32[16,3,16,1024]{3,2,1,0:T(8,128)S(1)}, f32[64,16,128]{2,1,0:T(8,128)S(1)}) custom-call(f32[16,3,16,1024]{3,2,1,0:T(8,128)} %a_hbm.1, f32[16,3,16,1024]{3,2,1,0:T(8,128)} %cx_hbm.3, f32[16,3,16,1024]{3,2,1,0:T(8,128)} %cy_hbm.3, bf16[1,64,16,512]{3,2,1,0:T(8,128)(2,1)S(1)} %copy-done.2, bf16[1,64,16]{2,1,0:T(8,128)(2,1)S(1)} %copy.8.innov, ...), custom_call_target="tpu_custom_call" | custom-call | tf_op jit(solution)/shard_map/sums_and_first_step/pallas_call | solution.py:511
  24.6 0.0 copy-start.1
  24.6 1.7 %copy-done.1 = f32[16,3,16,1024]{3,2,1,0:T(8,128)} copy-done((f32[16,3,16,1024]{3,2,1,0:T(8,128)}, f32[16,3,16,1024]{3,2,1,0:T(8,128)S(1)}, u32[]{:S(2)}) %copy-start.1) | copy-done | bytes 3145752
  26.2 28.3 %forcing.1.a_hbm = f32[16,3,16,1024]{3,2,1,0:T(8,128)S(1)} custom-call(f32[64,16,128]{2,1,0:T(8,128)S(1)} %get-tuple-element.7.recv, f32[16,3,16,1024]{3,2,1,0:T(8,128)} %copy-done.1), custom_call_target="tpu_custom_call" | custom-call | tf_op jit(solution)/shard_map/forcing/pallas_call | solution.py:527
  54.5 0.0 copy-start
  54.5 1.7 %copy-done = f32[16,3,16,1024]{3,2,1,0:T(8,128)} copy-done((f32[16,3,16,1024]{3,2,1,0:T(8,128)}, f32[16,3,16,1024]{3,2,1,0:T(8,128)S(1)}, u32[]{:S(2)}) %copy-start) | copy-done | bytes 3145752
  56.2 14.4 %second_step.1 = f32[16,3,16,1024]{3,2,1,0:T(8,128)S(1)} custom-call(f32[16,3,16,1024]{3,2,1,0:T(8,128)} %copy-done, f32[16,3,16,1024]{3,2,1,0:T(8,128)} %cx_hbm.3, f32[16,3,16,1024]{3,2,1,0:T(8,128)} %cy_hbm.3), custom_call_target="tpu_custom_call" | custom-call | tf_op jit(solution)/shard_map/second_step/pallas_call | solution.py:544
  70.6 1.7 %copy.12 = f32[16,3,16,1024]{3,2,1,0:T(8,128)} copy(f32[16,3,16,1024]{3,2,1,0:T(8,128)S(1)} %second_step.1) | data formatting | bytes 6291456
Async XLA Ops:
  2.3 1.2 %copy-start.2 = (bf16[1,64,16,512]{3,2,1,0:T(8,128)(2,1)S(1)}, bf16[1,64,16,512]{3,2,1,0:T(8,128)(2,1)}, u32[]{:S(2)}) copy-start(bf16[1,64,16,512]{3,2,1,0:T(8,128)(2,1)} %tiles.1) | copy-start | bytes 3145732
  24.6 1.7 %copy-start.1 = (f32[16,3,16,1024]{3,2,1,0:T(8,128)}, f32[16,3,16,1024]{3,2,1,0:T(8,128)S(1)}, u32[]{:S(2)}) copy-start(f32[16,3,16,1024]{3,2,1,0:T(8,128)S(1)} %get-tuple-element.8.dense_hbm) | copy-start | bytes 9437188
  54.5 1.7 %copy-start = (f32[16,3,16,1024]{3,2,1,0:T(8,128)}, f32[16,3,16,1024]{3,2,1,0:T(8,128)S(1)}, u32[]{:S(2)}) copy-start(f32[16,3,16,1024]{3,2,1,0:T(8,128)S(1)} %forcing.1.a_hbm) | copy-start | bytes 9437188

commit v2 on v1

v2 whole, which is shorter than its diff:
```python
import functools

import jax
import jax.numpy as jnp
from jax import lax
from jax.experimental import pallas as pl
from jax.experimental.pallas import tpu as pltpu
from jax.sharding import PartitionSpec as P

LEV, LF, RD, NC = 16, 3, 16, 1024
BANDS, RAYS, K, CAP = 64, 16, 32, 2
GROUP = 8
RELAYS = BANDS // GROUP
LANES = 128
PACK = 16
SENT = 9
COPIES = 4
F32, BF16, I32 = jnp.float32, jnp.bfloat16, jnp.int32
MESH = pl.DeviceIdType.MESH


def iota(shape, dim):
    return lax.broadcasted_iota(I32, shape, dim)


def dot(a, b):
    return jnp.dot(a, b, preferred_element_type=F32)


def dot_t(a, b):
    return lax.dot_general(a, b, (((1,), (1,)), ((), ())), preferred_element_type=F32)


def split(value):
    high = value.astype(BF16)
    rest = value - high.astype(F32)
    mid = rest.astype(BF16)
    return high, mid, rest - mid.astype(F32)


class Halo:
    def __init__(self, ups, sides, below, side_in, rot, sems):
        self.ups, self.sides, self.below, self.side_in, self.rot = ups, sides, below, side_in, rot
        self.send, self.recv, self.rot_send, self.fwd_send, self.rot_recv = sems
        self.g = lax.axis_index("face")
        self.b = lax.axis_index("rows")

    def greet(self, barrier):
        g, b = self.g, self.b

        def hello(face, band):
            pl.semaphore_signal(barrier, inc=1, device_id=(face, band), device_id_type=MESH)

        hello(1 - g, b)

        @pl.when(b < BANDS - 1)
        def _():
            hello(g, b + 1)

        @pl.when(b == BANDS - 1)
        def _():
            hello(g, 0)

        @pl.when((b == BANDS - 1) & (g == 0))
        def _():
            hello(1, 0)

        @pl.when((b & (GROUP - 1)) != 0)
        def _():
            hello(g, b & -GROUP)

        @pl.when((b & (GROUP - 1)) == 0)
        def _():
            hello(1 - g, 0)

        @pl.when(((b & (GROUP - 1)) == 0) & (g == 0) & (b != 0))
        def _():
            hello(0, 0)

        relay = ((b & (GROUP - 1)) == 0).astype(I32)
        origin = (b == 0).astype(I32)
        return 2 + relay * (GROUP - 1) + origin * (RELAYS + jnp.where(g == 0, RELAYS - 1, 1))

    def zero(self):
        g, b = self.g, self.b
        edge = jnp.zeros((LEV, 1, NC), F32)

        @pl.when(b == BANDS - 1)
        def _():
            @pl.when(g == 0)
            def _():
                self.below[:, 1] = edge

            @pl.when(g == 1)
            def _():
                self.below[:, 0] = edge
                self.below[:, 2] = edge

        @pl.when(g == 1)
        def _():
            self.rot[1] = jnp.zeros((LEV, 1, LANES), F32)

    def copy(self, src, dst, send, recv, face, band):
        return pltpu.make_async_remote_copy(
            src_ref=src, dst_ref=dst, send_sem=send, recv_sem=recv,
            device_id=(face, band), device_id_type=MESH,
        )

    def row(self, face):
        return self.copy(self.ups.at[:, :, 0:1, :], self.below, self.send.at[0], self.recv.at[0], self.g, face)

    def one(self, src, dst, face, slot):
        return self.copy(
            self.ups.at[:, src, 0:1, :], self.below.at[:, dst], self.send.at[slot], self.recv.at[slot], face, BANDS - 1
        )

    def side(self):
        return self.copy(self.sides, self.side_in, self.send.at[1], self.recv.at[1], 1 - self.g, self.b)

    def piece(self, src, dst, face, r, n):
        lanes = pl.ds(LANES * (RELAYS - 1 - r), LANES)
        return self.copy(
            self.ups.at[:, src, 0:1, lanes], self.rot.at[dst], self.rot_send.at[dst, r], self.rot_recv.at[dst],
            face, n,
        )

    def start(self):
        g, b = self.g, self.b

        @pl.when(b == 0)
        def _():
            @pl.when(g == 0)
            def _():
                for r in range(RELAYS):
                    self.piece(2, 0, 1, r, r * GROUP).start()
                for r in range(1, RELAYS):
                    self.piece(0, 1, 0, r, r * GROUP).start()
                self.one(1, 2, 0, 0).start()
                self.rot[1] = self.ups[:, 0, 0:1, NC - LANES :]

            @pl.when(g == 1)
            def _():
                for r in range(RELAYS):
                    self.piece(1, 0, 0, r, r * GROUP).start()
                self.one(0, 1, 1, 0).start()
                self.one(2, 0, 0, 2).start()

        @pl.when(b != 0)
        def _():
            self.row(b - 1).start()

        self.side().start()

    def forward(self, dst, i):
        return self.copy(
            self.rot.at[dst], self.rot.at[dst], self.fwd_send.at[dst, i], self.rot_recv.at[dst],
            self.g, (self.b & -GROUP) + i,
        )

    def relay(self):
        g, b = self.g, self.b

        @pl.when((b & (GROUP - 1)) == 0)
        def _():
            self.forward(0, 1).wait_recv()
            for i in range(1, GROUP):
                self.forward(0, i).start()

            @pl.when(g == 0)
            def _():
                @pl.when(b != 0)
                def _():
                    self.forward(1, 1).wait_recv()

                for i in range(1, GROUP):
                    self.forward(1, i).start()

    def wait_rotated(self):
        g, b = self.g, self.b

        @pl.when((b & (GROUP - 1)) != 0)
        def _():
            self.forward(0, 1).wait_recv()

            @pl.when(g == 0)
            def _():
                self.forward(1, 1).wait_recv()

    def wait_rows(self):
        g, b = self.g, self.b
        self.side().wait_recv()

        @pl.when(b != BANDS - 1)
        def _():
            self.row(0).wait_recv()

        @pl.when(b == BANDS - 1)
        def _():
            @pl.when(g == 0)
            def _():
                self.one(1, 2, 0, 0).wait_recv()
                self.one(2, 0, 0, 2).wait_recv()

            @pl.when(g == 1)
            def _():
                self.one(0, 1, 1, 0).wait_recv()

    def finish(self):
        g, b = self.g, self.b
        self.side().wait_send()

        @pl.when(b != 0)
        def _():
            self.row(0).wait_send()

        @pl.when(b == 0)
        def _():
            @pl.when(g == 0)
            def _():
                for r in range(RELAYS):
                    self.piece(2, 0, 1, r, r * GROUP).wait_send()
                for r in range(1, RELAYS):
                    self.piece(0, 1, 0, r, r * GROUP).wait_send()
                self.one(1, 2, 0, 0).wait_send()

            @pl.when(g == 1)
            def _():
                for r in range(RELAYS):
                    self.piece(1, 0, 0, r, r * GROUP).wait_send()
                self.one(0, 1, 1, 0).wait_send()
                self.one(2, 0, 0, 2).wait_send()

        @pl.when((b & (GROUP - 1)) == 0)
        def _():
            for i in range(1, GROUP):
                self.forward(0, i).wait_send()

            @pl.when(g == 0)
            def _():
                for i in range(1, GROUP):
                    self.forward(1, i).wait_send()


def halo_in():
    return [
        pltpu.VMEM((LEV, LF, 1, NC), F32),
        pltpu.VMEM((RD, LANES), F32),
        pltpu.VMEM((2, LEV, 1, LANES), F32),
        pltpu.SemaphoreType.DMA((3,)),
        pltpu.SemaphoreType.DMA((3,)),
        pltpu.SemaphoreType.DMA((2, RELAYS)),
        pltpu.SemaphoreType.DMA((2, GROUP)),
        pltpu.SemaphoreType.DMA((2,)),
    ]


UPS = (LEV, LF, 8, NC)
SIDES = (RD, LANES)
FIELD = (LEV, LF, RD, NC)


def west(a, cx, sides):
    along = cx[:, 0, :, 0:LANES] * a[:, 0, :, 0:LANES]
    lane = iota(SIDES, 1)
    total = jnp.zeros(SIDES, F32)
    for l in range(LEV):
        total = jnp.where(lane == l, jnp.broadcast_to(along[l, :, 0:1], SIDES), total)
    sides[...] = total


def interior(a, cx, cy, out, lo, hi):
    row = iota((RD, NC), 0)
    col = iota((RD, NC), 1)

    def body(l, carry):
        base, rolled = [], []
        for f in range(LF):
            value, x, y = a[l, f], cx[l, f], cy[l, f]
            along, upward = x * value, y * value
            rolled.append(pltpu.roll(along, NC - 1, 1))
            lifted = jnp.where(row < RD - 1, pltpu.roll(upward, RD - 1, 0), 0.0)
            base.append((1.0 - x - y) * value + lifted)
        for f in range(LF):
            beyond = rolled[f + 1] if f + 1 < LF else 0.0
            out[l, f] = base[f] + jnp.where(col < NC - 1, rolled[f], beyond)
        return carry

    lax.fori_loop(lo, hi, body, 0)


def patch_rows(out, below, side_in):
    def body(l, carry):
        for f in range(LF):
            out[l, f, RD - 1 : RD, :] += below[l, f]
        return carry

    lax.fori_loop(0, LEV, body, 0)
    full = (LEV, RD, LANES)
    lane = iota(full, 2)
    mine = jnp.where(lane == iota(full, 0), jnp.broadcast_to(side_in[...][None], full), 0.0)
    right = jnp.sum(mine, axis=2, keepdims=True)
    out[:, 2, :, NC - LANES :] += jnp.where(lane == LANES - 1, right, 0.0)


def patch_rotated(out, rot):
    g = lax.axis_index("face")
    b = lax.axis_index("rows")
    full = (LEV, RD, LANES)
    lane = iota(full, 2)
    place = LANES - 1 - RD * (b & (GROUP - 1)) - iota(full, 1)

    def column(piece):
        picked = jnp.where(lane == place, jnp.broadcast_to(piece, full), 0.0)
        return jnp.where(lane == 0, jnp.sum(picked, axis=2, keepdims=True), 0.0)

    out[:, pl.ds(g, 1), :, 0:LANES] += column(rot[0]).reshape(LEV, 1, RD, LANES)

    @pl.when(g == 0)
    def _():
        out[:, 2, :, 0:LANES] += column(rot[1])


def pack(tiles, innov, dest, cells, send):
    blocks = BANDS
    wide = blocks * RAYS
    ray = iota((RAYS, wide), 1) & (RAYS - 1)
    repeat = (lax.shift_right_logical(iota((blocks, wide), 1), 4) == iota((blocks, wide), 0)).astype(BF16)
    lines = jnp.where(ray == iota((RAYS, wide), 0), dot(innov[0], repeat), 0.0)
    weight = jnp.sum(lines, axis=0, keepdims=True)

    square = (blocks, blocks)
    first, second = iota(square, 0), iota(square, 1)
    target = jnp.broadcast_to(dest[0].astype(F32), square)
    other = dot(jnp.where(first == second, target, 0.0).astype(BF16), jnp.ones(square, BF16))
    same = (other == target) & (first < second)
    order = jnp.sum(same.astype(F32), axis=0, keepdims=True)
    slot = iota((CAP * BANDS, blocks), 0)
    band = ((slot + lax.axis_index("rows")) & (BANDS - 1)).astype(F32)
    turn = lax.shift_right_logical(slot, 6).astype(F32)
    chosen = ((band == target[0:1]) & (turn == order)).astype(BF16)

    sums = dot((dot(chosen, repeat) * weight).astype(BF16), tiles[0].reshape(wide, LEV * K))
    src, dst = iota((LEV * K, LEV * K), 0), iota((LEV * K, LEV * K), 1)
    level = lax.shift_right_logical(dst & (LANES - 1), 3)
    part = lax.shift_right_logical(dst, 7)
    mixed = (src == level * K + part * 8 + (dst & 7)).astype(BF16)
    high, mid, low = split(sums)
    sums = dot(high, mixed) + dot(mid, mixed) + dot(low.astype(BF16), mixed)

    cell = cells[0]
    shift = lax.shift_right_logical
    code = ((shift(cell, 13) * NC + (cell & (NC - 1))) * 8) + (shift(cell, 10) & 7)
    upper, lower = shift(code, 8).astype(F32).astype(BF16), (code & 255).astype(F32).astype(BF16)
    codes = dot_t(chosen, upper) * 256.0 + dot_t(chosen, lower)
    codes = jnp.concatenate(
        [codes[:BANDS], codes[BANDS:], jnp.zeros((BANDS, LANES - 2 * K), F32)], axis=1
    )
    flat = send.reshape(BANDS * PACK, LANES)
    for s in range(CAP):
        for q in range(4):
            flat[pl.ds(s * 4 + q, BANDS, stride=PACK), :] = sums[
                s * BANDS : (s + 1) * BANDS, q * LANES : (q + 1) * LANES
            ]
    flat[pl.ds(SENT - 1, BANDS, stride=PACK), :] = codes


def first_kernel(
    a_hbm, cx_hbm, cy_hbm, tiles_hbm, innov_hbm, dest_hbm, cells_hbm, out, recv, cx, cy,
    a, tiles, innov, dest, cells, send, load_sem, pack_send, pack_recv, own_sem, ups, sides,
    below, side_in, rot, *sems,
):
    g = lax.axis_index("face")
    b = lax.axis_index("rows")
    pairs = (
        (innov_hbm, innov), (dest_hbm, dest), (cells_hbm, cells), (tiles_hbm, tiles),
        (a_hbm, a), (cy_hbm, cy), (cx_hbm, cx),
    )
    loads = [pltpu.make_async_copy(src, dst, load_sem.at[i]) for i, (src, dst) in enumerate(pairs)]
    for load in loads:
        load.start()
    halo = Halo(ups, sides, below, side_in, rot, sems)
    barrier = pltpu.get_barrier_semaphore()
    expected = halo.greet(barrier) + BANDS - 1

    def hello(i, carry):
        pl.semaphore_signal(barrier, inc=1, device_id=(g, (b + i) & (BANDS - 1)), device_id_type=MESH)
        return carry

    lax.fori_loop(1, BANDS, hello, 0)
    halo.zero()
    for load in loads[:4]:
        load.wait()
    pack(tiles, innov, dest, cells, send)
    own = pltpu.make_async_copy(send.at[0, pl.ds(0, SENT)], recv.at[0, pl.ds(0, SENT)], own_sem)
    own.start()
    for load in loads[4:]:
        load.wait()

    def lift(l, carry):
        ups[l] = cy[l, :, 0:8, :] * a[l, :, 0:8, :]
        return carry

    lax.fori_loop(0, LEV, lift, 0)
    west(a, cx, sides)
    pl.semaphore_wait(barrier, expected)
    halo.start()

    def packets(which, band):
        return pltpu.make_async_remote_copy(
            src_ref=send.at[which, pl.ds(0, SENT)],
            dst_ref=recv.at[which, pl.ds(0, SENT)],
            send_sem=pack_send,
            recv_sem=pack_recv,
            device_id=(g, band),
            device_id_type=MESH,
        )

    def ship(i, carry):
        packets(i, (b + i) & (BANDS - 1)).start()
        return carry

    lax.fori_loop(1, BANDS, ship, 0)
    halo.relay()
    interior(a, cx, cy, out, 0, LEV)
    halo.wait_rows()
    patch_rows(out, below, side_in)
    halo.wait_rotated()
    patch_rotated(out, rot)
    halo.finish()
    own.wait()
    packets(pl.ds(1, BANDS - 1), b).wait()


def scatter_kernel(recv, dense, cx, cy, out, ups, sides, index, index_s, values, *rest):
    fields, (index_sem,) = rest[:COPIES], rest[COPIES:]
    flat = recv.reshape(BANDS * PACK, LANES)
    index[...] = flat[pl.ds(SENT - 1, BANDS, stride=PACK), :].astype(I32)
    to_scalar = pltpu.make_async_copy(index, index_s, index_sem)
    to_scalar.start()

    shift = lax.shift_right_logical
    from_lane, to_lane = iota((2 * LANES, 8 * LANES), 0), iota((2 * LANES, 8 * LANES), 1)
    from_lane = from_lane & (LANES - 1)
    widen = (shift(from_lane, 3) == shift(to_lane & (LANES - 1), 3)) & ((from_lane & 7) == shift(to_lane, 7))
    widen = widen.astype(F32).astype(BF16)
    got = recv[:, 0 : CAP * 4, :].reshape(BANDS * CAP * 4, LANES)
    high, mid, _ = split(got)
    wide = dot(jnp.concatenate([high, mid], axis=1), widen)
    values[...] = wide.reshape(BANDS, CAP * 4, 8 * LANES)

    def clear(i, carry):
        for field in fields:
            field[pl.ds(i * LANES, LANES), :] = jnp.zeros((LANES, LANES), F32)
        return carry

    lax.fori_loop(0, LF * 2 * NC // LANES, clear, 0)
    to_scalar.wait()
    lane = iota((1, LANES), 1) & 7

    def add(i, carry):
        for e in range(CAP * K):
            code = index_s[i, e]
            line = values[i, e // 8 : e // 8 + 1, e % 8 * LANES : (e % 8 + 1) * LANES]
            field = fields[e % COPIES]
            field[pl.ds(shift(code, 3), 1), :] += jnp.where(lane == (code & 7), line, 0.0)
        return carry

    lax.fori_loop(0, BANDS, add, 0)

    def turn(f, carry):
        for half in range(2):
            for c in range(NC // LANES):
                rows = pl.ds((f * 2 + half) * NC + c * LANES, LANES)
                block = sum(field[rows, :] for field in fields)
                turned = block.T.reshape(LEV, 8, LANES)
                cols = slice(c * LANES, (c + 1) * LANES)
                value = dense[:, f, half * 8 : half * 8 + 8, cols] + turned
                out[:, f, half * 8 : half * 8 + 8, cols] = value
                if half == 0:
                    ups[:, f, :, cols] = cy[:, f, 0:8, cols] * value
        return carry

    lax.fori_loop(0, LF, turn, 0)
    west(out, cx, sides)


def last_kernel(a, cx, cy, ups, sides, out, below, side_in, rot, *sems):
    halo = Halo(ups, sides, below, side_in, rot, sems)
    barrier = pltpu.get_barrier_semaphore()
    expected = halo.greet(barrier)
    halo.zero()
    pl.semaphore_wait(barrier, expected)
    halo.start()
    interior(a, cx, cy, out, 0, LEV)
    halo.relay()
    halo.wait_rows()
    patch_rows(out, below, side_in)
    halo.wait_rotated()
    patch_rotated(out, rot)
    halo.finish()


def params(mib, cid=None):
    kw = {} if cid is None else dict(collective_id=cid, has_side_effects=True)
    return pltpu.CompilerParams(vmem_limit_bytes=mib * 1024 * 1024, **kw)


def per_device(final_adjoint, courant_x, courant_y, ray_tiles, ray_innov, ray_dest, ray_cols):
    vmem, anywhere = pl.BlockSpec(memory_space=pltpu.VMEM), pl.BlockSpec(memory_space=pl.ANY)
    field = jax.ShapeDtypeStruct(FIELD, F32)
    dma = pltpu.SemaphoreType.DMA
    dense, recv, held_x, held_y = pl.pallas_call(
        first_kernel,
        out_shape=(field, jax.ShapeDtypeStruct((BANDS, PACK, LANES), F32), field, field),
        in_specs=[pl.BlockSpec(memory_space=pltpu.HBM)] * 7,
        out_specs=(vmem, anywhere, vmem, vmem),
        scratch_shapes=[
            pltpu.VMEM(FIELD, F32),
            pltpu.VMEM((1, BANDS, RAYS, LEV * K), BF16),
            pltpu.VMEM((1, RAYS, BANDS), BF16),
            pltpu.VMEM((1, 1, BANDS), I32),
            pltpu.VMEM((1, K, BANDS), I32),
            pltpu.VMEM((BANDS, PACK, LANES), F32),
            dma((7,)), dma, dma, dma,
            pltpu.VMEM(UPS, F32),
            pltpu.VMEM(SIDES, F32),
        ] + halo_in(),
        compiler_params=params(28, 0),
        name="sums_and_first_step",
    )(*(
        pltpu.with_memory_space_constraint(value, pltpu.HBM)
        for value in (
            final_adjoint, courant_x, courant_y, ray_tiles,
            jnp.swapaxes(ray_innov, 1, 2), jnp.swapaxes(ray_dest, 1, 2), jnp.swapaxes(ray_cols, 1, 2),
        )
    ))
    mid, ups, sides = pl.pallas_call(
        scatter_kernel,
        out_shape=(field, jax.ShapeDtypeStruct(UPS, F32), jax.ShapeDtypeStruct(SIDES, F32)),
        in_specs=[vmem] * 4,
        out_specs=(vmem, vmem, vmem),
        scratch_shapes=[
            pltpu.VMEM((BANDS, LANES), I32),
            pltpu.SMEM((BANDS, LANES), I32),
            pltpu.VMEM((BANDS, CAP * 4, 8 * LANES), F32),
        ] + [pltpu.VMEM((LF * 2 * NC, LANES), F32)] * COPIES + [dma],
        compiler_params=params(36),
        name="forcing",
    )(recv, dense, held_x, held_y)
    return pl.pallas_call(
        last_kernel,
        out_shape=field,
        in_specs=[vmem] * 5,
        out_specs=vmem,
        scratch_shapes=halo_in(),
        compiler_params=params(28, 1),
        name="second_step",
    )(mid, held_x, held_y, ups, sides)


def solution(mesh):
    placed = (
        P(None, "face", "rows", None),
        P(None, "face", "rows", None),
        P(None, "face", "rows", None),
        P("face", "rows", None, None),
        P("face", "rows", None),
        P("face", "rows", None),
        P("face", "rows", None),
    )
    return jax.shard_map(
        per_device,
        mesh=mesh,
        in_specs=placed,
        out_specs=P(None, "face", "rows", None),
        check_vma=False,
    )
```

time: 72.5 us -> 41.5 us (0.57)
  Pallas kernels: 63.7 us -> 39.7 us
  local copies, waits for them, and re-layouts: 8.53 us -> 1.67 us
    pallas_call x2, Pallas kernels: 42.7 us -> 23.3 us  [the longest x1 13.7 us: per_device(): pl.pallas_call(last_kernel, out_shape=field, in_specs=[vmem] * 5, out_spe...]
    unnamed x10 -> x1, local copies, waits for them, and re-layouts: 8.53 us -> 1.67 us
    pallas_call x1, Pallas kernels: 21 us -> 16.4 us  [per_device(): pl.pallas_call(first_kernel, out_shape=(field, jax.ShapeDtypeStruct((BAND...]
where the time goes in v2:
time: 41.5 us; the launch traced here: 41.4 us
  Pallas kernels  39.7 us (96%)
  local copies, waits for them, and re-layouts  1.67 us (4%)
    pallas_call x1, Pallas kernels, per_device(): pl.pallas_call(first_kernel, out_shape=(field, jax.ShapeDtypeStruct((BAND...  16.4 us
    pallas_call x1, Pallas kernels, per_device(): pl.pallas_call(last_kernel, out_shape=field, in_specs=[vmem] * 5, out_spe...  13.7 us
    pallas_call x1, Pallas kernels, per_device(): pl.pallas_call(scatter_kernel, out_shape=(field, jax.ShapeDtypeStruct(UPS...  9.58 us
    unnamed x1, local copies, waits for them, and re-layouts  1.67 us

profile of v2, /device:TPU:27, one launch (start us, length us, event | category | flops | bytes accessed | tf_op | source)
XLA Modules:
  0.0 41.4 jit_solution(17856695142160759960)
XLA Ops:
  0.0 16.4 %sums_and_first_step.1 = (f32[16,3,16,1024]{3,2,1,0:T(8,128)S(1)}, f32[64,16,128]{2,1,0:T(8,128)S(1)}, f32[16,3,16,1024]{3,2,1,0:T(8,128)S(1)}, f32[16,3,16,1024]{3,2,1,0:T(8,128)S(1)}) custom-call(f32[16,3,16,1024]{3,2,1,0:T(8,128)} %a_hbm.1, f32[16,3,16,1024]{3,2,1,0:T(8,128)} %cx_hbm.1, f32[16,3,16,1024]{3,2,1,0:T(8,128)} %cy_hbm.1, ...), custom_call_target="tpu_custom_call" | custom-call | tf_op jit(solution)/shard_map/sums_and_first_step/pallas_call | solution.py:512
  16.4 9.6 %forcing.1 = (f32[16,3,16,1024]{3,2,1,0:T(8,128)S(1)}, f32[16,3,8,1024]{3,2,1,0:T(8,128)S(1)}, f32[16,128]{1,0:T(8,128)S(1)}) custom-call(f32[64,16,128]{2,1,0:T(8,128)S(1)} %get-tuple-element.12.recv, f32[16,3,16,1024]{3,2,1,0:T(8,128)S(1)} %get-tuple-element.13.dense, f32[16,3,16,1024]{3,2,1,0:T(8,128)S(1)} %get-tuple-element.14.cx, ...), custom_call_target="tpu_custom_call" | custom-call | tf_op jit(solution)/shard_map/forcing/pallas_call | solution.py:537
  26.0 13.7 %second_step.1 = f32[16,3,16,1024]{3,2,1,0:T(8,128)S(1)} custom-call(f32[16,3,16,1024]{3,2,1,0:T(8,128)S(1)} %get-tuple-element.16.a, f32[16,3,16,1024]{3,2,1,0:T(8,128)S(1)} %get-tuple-element.14.cx, f32[16,3,16,1024]{3,2,1,0:T(8,128)S(1)} %get-tuple-element.15.cy, f32[16,3,8,1024]{3,2,1,0:T(8,128)S(1)} %get-tuple-element.17.ups, ...), custom_call_target="tpu_custom_call" | custom-call | tf_op jit(solution)/shard_map/second_step/pallas_call | solution.py:550
  39.7 1.7 %copy.9 = f32[16,3,16,1024]{3,2,1,0:T(8,128)} copy(f32[16,3,16,1024]{3,2,1,0:T(8,128)S(1)} %second_step.1) | data formatting | bytes 6291456

commit v3 on v2

--- a/solution.py
+++ b/solution.py
@@ -14,7 +14,6 @@
 LANES = 128
 PACK = 16
 SENT = 9
-COPIES = 4
 F32, BF16, I32 = jnp.float32, jnp.bfloat16, jnp.int32
 MESH = pl.DeviceIdType.MESH
 
@@ -39,8 +38,8 @@
 
 
 class Halo:
-    def __init__(self, ups, sides, below, side_in, rot, sems):
-        self.ups, self.sides, self.below, self.side_in, self.rot = ups, sides, below, side_in, rot
+    def __init__(self, ups, sides, seam, below, side_in, rot, sems):
+        self.ups, self.sides, self.seam, self.below, self.side_in, self.rot = ups, sides, seam, below, side_in, rot
         self.send, self.recv, self.rot_send, self.fwd_send, self.rot_recv = sems
         self.g = lax.axis_index("face")
         self.b = lax.axis_index("rows")
@@ -98,7 +97,7 @@
 
         @pl.when(g == 1)
         def _():
-            self.rot[1] = jnp.zeros((LEV, 1, LANES), F32)
+            self.rot[1] = jnp.zeros((LEV, LANES), F32)
 
     def copy(self, src, dst, send, recv, face, band):
         return pltpu.make_async_remote_copy(
@@ -117,11 +116,11 @@
     def side(self):
         return self.copy(self.sides, self.side_in, self.send.at[1], self.recv.at[1], 1 - self.g, self.b)
 
-    def piece(self, src, dst, face, r, n):
+    def piece(self, which, face, r, n):
         lanes = pl.ds(LANES * (RELAYS - 1 - r), LANES)
         return self.copy(
-            self.ups.at[:, src, 0:1, lanes], self.rot.at[dst], self.rot_send.at[dst, r], self.rot_recv.at[dst],
-            face, n,
+            self.seam.at[which, :, lanes], self.rot.at[which],
+            self.rot_send.at[which, r], self.rot_recv.at[which], face, n,
         )
 
     def start(self):
@@ -131,25 +130,28 @@
         def _():
             @pl.when(g == 0)
             def _():
+                for l in range(LEV):
+                    self.seam[0, l : l + 1, :] = self.ups[l, 2, 0:1, :]
+                    self.seam[1, l : l + 1, :] = self.ups[l, 0, 0:1, :]
                 for r in range(RELAYS):
-                    self.piece(2, 0, 1, r, r * GROUP).start()
+                    self.piece(0, 1, r, r * GROUP).start()
                 for r in range(1, RELAYS):
-                    self.piece(0, 1, 0, r, r * GROUP).start()
+                    self.piece(1, 0, r, r * GROUP).start()
                 self.one(1, 2, 0, 0).start()
-                self.rot[1] = self.ups[:, 0, 0:1, NC - LANES :]
+                self.rot[1] = self.seam[1, :, NC - LANES :]
 
             @pl.when(g == 1)
             def _():
+                for l in range(LEV):
+                    self.seam[0, l : l + 1, :] = self.ups[l, 1, 0:1, :]
                 for r in range(RELAYS):
-                    self.piece(1, 0, 0, r, r * GROUP).start()
+                    self.piece(0, 0, r, r * GROUP).start()
                 self.one(0, 1, 1, 0).start()
                 self.one(2, 0, 0, 2).start()
 
         @pl.when(b != 0)
         def _():
             self.row(b - 1).start()
-
-        self.side().start()
 
     def forward(self, dst, i):
         return self.copy(
@@ -188,7 +190,6 @@
 
     def wait_rows(self):
         g, b = self.g, self.b
-        self.side().wait_recv()
 
         @pl.when(b != BANDS - 1)
         def _():
@@ -218,15 +219,15 @@
             @pl.when(g == 0)
             def _():
                 for r in range(RELAYS):
-                    self.piece(2, 0, 1, r, r * GROUP).wait_send()
+                    self.piece(0, 1, r, r * GROUP).wait_send()
                 for r in range(1, RELAYS):
-                    self.piece(0, 1, 0, r, r * GROUP).wait_send()
+                    self.piece(1, 0, r, r * GROUP).wait_send()
                 self.one(1, 2, 0, 0).wait_send()
 
             @pl.when(g == 1)
             def _():
                 for r in range(RELAYS):
-                    self.piece(1, 0, 0, r, r * GROUP).wait_send()
+                    self.piece(0, 0, r, r * GROUP).wait_send()
                 self.one(0, 1, 1, 0).wait_send()
                 self.one(2, 0, 0, 2).wait_send()
 
@@ -241,11 +242,19 @@
                     self.forward(1, i).wait_send()
 
 
-def halo_in():
+def landing():
     return [
-        pltpu.VMEM((LEV, LF, 1, NC), F32),
-        pltpu.VMEM((RD, LANES), F32),
-        pltpu.VMEM((2, LEV, 1, LANES), F32),
+        (LEV, LF, 1, NC),
+        (RD, LANES),
+        (2, LEV, LANES),
+    ]
+
+
+def halo_scratch():
+    return [
+        pltpu.VMEM(UPS, F32),
+        pltpu.VMEM(SIDES, F32),
+        pltpu.VMEM((2, LEV, NC), F32),
         pltpu.SemaphoreType.DMA((3,)),
         pltpu.SemaphoreType.DMA((3,)),
         pltpu.SemaphoreType.DMA((2, RELAYS)),
@@ -259,8 +268,7 @@
 FIELD = (LEV, LF, RD, NC)
 
 
-def west(a, cx, sides):
-    along = cx[:, 0, :, 0:LANES] * a[:, 0, :, 0:LANES]
+def west(along, sides):
     lane = iota(SIDES, 1)
     total = jnp.zeros(SIDES, F32)
     for l in range(LEV):
@@ -288,36 +296,37 @@
     lax.fori_loop(lo, hi, body, 0)
 
 
-def patch_rows(out, below, side_in):
+def patch_rows(out, below, side_in, lo, hi):
     def body(l, carry):
         for f in range(LF):
             out[l, f, RD - 1 : RD, :] += below[l, f]
         return carry
 
-    lax.fori_loop(0, LEV, body, 0)
-    full = (LEV, RD, LANES)
+    lax.fori_loop(lo, hi, body, 0)
+    full = (hi - lo, RD, LANES)
     lane = iota(full, 2)
-    mine = jnp.where(lane == iota(full, 0), jnp.broadcast_to(side_in[...][None], full), 0.0)
+    mine = jnp.where(lane == iota(full, 0) + lo, jnp.broadcast_to(side_in[...][None], full), 0.0)
     right = jnp.sum(mine, axis=2, keepdims=True)
-    out[:, 2, :, NC - LANES :] += jnp.where(lane == LANES - 1, right, 0.0)
-
-
-def patch_rotated(out, rot):
+    out[lo:hi, 2, :, NC - LANES :] += jnp.where(lane == LANES - 1, right, 0.0)
+
+
+def patch_rotated(out, rot, lo, hi):
     g = lax.axis_index("face")
     b = lax.axis_index("rows")
-    full = (LEV, RD, LANES)
+    full = (hi - lo, RD, LANES)
     lane = iota(full, 2)
     place = LANES - 1 - RD * (b & (GROUP - 1)) - iota(full, 1)
 
-    def column(piece):
-        picked = jnp.where(lane == place, jnp.broadcast_to(piece, full), 0.0)
+    def column(which):
+        piece = rot[which, lo:hi, :]
+        picked = jnp.where(lane == place, jnp.broadcast_to(piece[:, None, :], full), 0.0)
         return jnp.where(lane == 0, jnp.sum(picked, axis=2, keepdims=True), 0.0)
 
-    out[:, pl.ds(g, 1), :, 0:LANES] += column(rot[0]).reshape(LEV, 1, RD, LANES)
+    out[lo:hi, pl.ds(g, 1), :, 0:LANES] += column(0).reshape(hi - lo, 1, RD, LANES)
 
     @pl.when(g == 0)
     def _():
-        out[:, 2, :, 0:LANES] += column(rot[1])
+        out[lo:hi, 2, :, 0:LANES] += column(1)
 
 
 def pack(tiles, innov, dest, cells, send):
@@ -341,16 +350,15 @@
 
     sums = dot((dot(chosen, repeat) * weight).astype(BF16), tiles[0].reshape(wide, LEV * K))
     src, dst = iota((LEV * K, LEV * K), 0), iota((LEV * K, LEV * K), 1)
-    level = lax.shift_right_logical(dst & (LANES - 1), 3)
+    inner = lax.shift_right_logical(dst & (LANES - 1), 4)
     part = lax.shift_right_logical(dst, 7)
-    mixed = (src == level * K + part * 8 + (dst & 7)).astype(BF16)
+    mixed = (src == (dst & (LEV - 1)) * K + part * 8 + inner).astype(BF16)
     high, mid, low = split(sums)
     sums = dot(high, mixed) + dot(mid, mixed) + dot(low.astype(BF16), mixed)
 
     cell = cells[0]
-    shift = lax.shift_right_logical
-    code = ((shift(cell, 13) * NC + (cell & (NC - 1))) * 8) + (shift(cell, 10) & 7)
-    upper, lower = shift(code, 8).astype(F32).astype(BF16), (code & 255).astype(F32).astype(BF16)
+    upper = lax.shift_right_logical(cell, 8).astype(F32).astype(BF16)
+    lower = (cell & 255).astype(F32).astype(BF16)
     codes = dot_t(chosen, upper) * 256.0 + dot_t(chosen, lower)
     codes = jnp.concatenate(
         [codes[:BANDS], codes[BANDS:], jnp.zeros((BANDS, LANES - 2 * K), F32)], axis=1
@@ -364,10 +372,61 @@
     flat[pl.ds(SENT - 1, BANDS, stride=PACK), :] = codes
 
 
+HALF = BANDS // 2
+DEPTH = HALF * CAP * K
+WIDE = 256
+
+
+def one_hots(recv, first, left, right, top):
+    flat = recv.reshape(BANDS * PACK, LANES)
+    at = first * PACK
+    codes = flat[pl.ds(at + SENT - 1, HALF, stride=PACK), :]
+    face_row = iota((LF * RD, LANES), 0)
+    column = iota((LANES, NC), 1)
+    size = LEV * LF * RD
+    for pair in range(2):
+        spots = [(s, 2 * pair + half) for half in range(2) for s in range(CAP)]
+        sums = jnp.concatenate(
+            [flat[pl.ds(at + s * 4 + q, HALF, stride=PACK), :] for s, q in spots], axis=0
+        ).T
+        cells = jnp.concatenate(
+            [pltpu.roll(codes, (LANES - s * K - q * 8) % LANES, 1) for s, q in spots], axis=0
+        )
+        rows = lax.shift_right_logical(cells.T.astype(I32), 10)
+        cols = cells.astype(I32) & (NC - 1)
+        for inner in range(8):
+            part = slice((pair * 8 + inner) * LANES, (pair * 8 + inner + 1) * LANES)
+            high, mid, _ = split(sums[inner * LEV : (inner + 1) * LEV])
+            row = rows[inner : inner + 1]
+            chosen = jnp.where(face_row == row, 1.0, 0.0).astype(BF16)
+            for n, term in enumerate((high, mid)):
+                product = term[:, None, :] * chosen[None]
+                left[n * size : (n + 1) * size, part] = product.reshape(size, LANES)
+                if top is not None:
+                    for f in range(LF):
+                        kept = jnp.where(row == f * RD, term.astype(F32), 0.0).astype(BF16)
+                        top[(n * LF + f) * LEV : (n * LF + f + 1) * LEV, part] = kept
+            right[part, :] = jnp.where(column == cols[:, inner : inner + 1], 1.0, 0.0).astype(BF16)
+
+
+def add_product(left, right, out, lo, hi):
+    size = LEV * LF * RD
+
+    def body(n, carry):
+        cols = pl.ds(pl.multiple_of(n * WIDE, WIDE), WIDE)
+        both = dot(left[...], right[:, cols])
+        out[:, :, :, cols] += (both[:size] + both[size:]).reshape(LEV, LF, RD, WIDE)
+        return carry
+
+    lax.fori_loop(lo, hi, body, 0)
+
+
 def first_kernel(
-    a_hbm, cx_hbm, cy_hbm, tiles_hbm, innov_hbm, dest_hbm, cells_hbm, out, recv, cx, cy,
-    a, tiles, innov, dest, cells, send, load_sem, pack_send, pack_recv, own_sem, ups, sides,
-    below, side_in, rot, *sems,
+    a_hbm, cx_hbm, cy_hbm, tiles_hbm, innov_hbm, dest_hbm, cells_hbm,
+    out, cx, cy, below2, side_in2, rot2,
+    a, tiles, innov, dest, cells, send, recv, left, right, top, load_sem, pack_send, pack_recv, own_sem,
+    below, side_in, rot, ups, sides, seam, sem1, sem2, sem3, sem4, sem5,
+    ups2, sides2, seam2, *sems2,
 ):
     g = lax.axis_index("face")
     b = lax.axis_index("rows")
@@ -378,7 +437,8 @@
     loads = [pltpu.make_async_copy(src, dst, load_sem.at[i]) for i, (src, dst) in enumerate(pairs)]
     for load in loads:
         load.start()
-    halo = Halo(ups, sides, below, side_in, rot, sems)
+    halo = Halo(ups, sides, seam, below, side_in, rot, (sem1, sem2, sem3, sem4, sem5))
+    halo2 = Halo(ups2, sides2, seam2, below2, side_in2, rot2, sems2)
     barrier = pltpu.get_barrier_semaphore()
     expected = halo.greet(barrier) + BANDS - 1
 
@@ -388,6 +448,7 @@
 
     lax.fori_loop(1, BANDS, hello, 0)
     halo.zero()
+    halo2.zero()
     for load in loads[:4]:
         load.wait()
     pack(tiles, innov, dest, cells, send)
@@ -401,103 +462,77 @@
         return carry
 
     lax.fori_loop(0, LEV, lift, 0)
-    west(a, cx, sides)
+    west(cx[:, 0, :, 0:LANES] * a[:, 0, :, 0:LANES], sides)
     pl.semaphore_wait(barrier, expected)
     halo.start()
-
-    def packets(which, band):
+    halo.side().start()
+
+    def packets(which, half, band):
         return pltpu.make_async_remote_copy(
             src_ref=send.at[which, pl.ds(0, SENT)],
             dst_ref=recv.at[which, pl.ds(0, SENT)],
             send_sem=pack_send,
-            recv_sem=pack_recv,
+            recv_sem=pack_recv.at[half],
             device_id=(g, band),
             device_id_type=MESH,
         )
 
-    def ship(i, carry):
-        packets(i, (b + i) & (BANDS - 1)).start()
-        return carry
-
-    lax.fori_loop(1, BANDS, ship, 0)
+    for half in range(2):
+
+        def ship(i, carry, half=half):
+            packets(i, half, (b + i) & (BANDS - 1)).start()
+            return carry
+
+        lax.fori_loop(max(1, half * HALF), (half + 1) * HALF, ship, 0)
     halo.relay()
     interior(a, cx, cy, out, 0, LEV)
+    own.wait()
+    packets(pl.ds(1, HALF - 1), 0, b).wait_recv()
+    one_hots(recv, 0, left, right, None)
+    add_product(left, right, out, 0, NC // WIDE)
     halo.wait_rows()
-    patch_rows(out, below, side_in)
+    halo.side().wait_recv()
+    patch_rows(out, below, side_in, 0, LEV)
     halo.wait_rotated()
-    patch_rotated(out, rot)
+    patch_rotated(out, rot, 0, LEV)
+    packets(pl.ds(HALF, HALF), 1, b).wait_recv()
+    one_hots(recv, HALF, left, right, top)
+    first = dot(top[...], right[...])
+    first = first[: LF * LEV] + first[LF * LEV :]
+    for l in range(LEV):
+        for f in range(LF):
+            value = out[l, f, 0:1, :] + first[f * LEV + l : f * LEV + l + 1]
+            ups2[l, f, 0:1, :] = cy[l, f, 0:1, :] * value
+    halo2.start()
+    add_product(left, right, out, 0, 1)
+    west(cx[:, 0, :, 0:LANES] * out[:, 0, :, 0:LANES], sides2)
+    halo2.side().start()
+    add_product(left, right, out, 1, 2)
+    halo2.relay()
+    add_product(left, right, out, 2, NC // WIDE)
+    halo2.wait_rows()
+    halo2.side().wait_recv()
+    halo2.wait_rotated()
     halo.finish()
-    own.wait()
-    packets(pl.ds(1, BANDS - 1), b).wait()
-
-
-def scatter_kernel(recv, dense, cx, cy, out, ups, sides, index, index_s, values, *rest):
-    fields, (index_sem,) = rest[:COPIES], rest[COPIES:]
-    flat = recv.reshape(BANDS * PACK, LANES)
-    index[...] = flat[pl.ds(SENT - 1, BANDS, stride=PACK), :].astype(I32)
-    to_scalar = pltpu.make_async_copy(index, index_s, index_sem)
-    to_scalar.start()
-
-    shift = lax.shift_right_logical
-    from_lane, to_lane = iota((2 * LANES, 8 * LANES), 0), iota((2 * LANES, 8 * LANES), 1)
-    from_lane = from_lane & (LANES - 1)
-    widen = (shift(from_lane, 3) == shift(to_lane & (LANES - 1), 3)) & ((from_lane & 7) == shift(to_lane, 7))
-    widen = widen.astype(F32).astype(BF16)
-    got = recv[:, 0 : CAP * 4, :].reshape(BANDS * CAP * 4, LANES)
-    high, mid, _ = split(got)
-    wide = dot(jnp.concatenate([high, mid], axis=1), widen)
-    values[...] = wide.reshape(BANDS, CAP * 4, 8 * LANES)
-
-    def clear(i, carry):
-        for field in fields:
-            field[pl.ds(i * LANES, LANES), :] = jnp.zeros((LANES, LANES), F32)
-        return carry
-
-    lax.fori_loop(0, LF * 2 * NC // LANES, clear, 0)
-    to_scalar.wait()
-    lane = iota((1, LANES), 1) & 7
-
-    def add(i, carry):
-        for e in range(CAP * K):
-            code = index_s[i, e]
-            line = values[i, e // 8 : e // 8 + 1, e % 8 * LANES : (e % 8 + 1) * LANES]
-            field = fields[e % COPIES]
-            field[pl.ds(shift(code, 3), 1), :] += jnp.where(lane == (code & 7), line, 0.0)
-        return carry
-
-    lax.fori_loop(0, BANDS, add, 0)
-
-    def turn(f, carry):
-        for half in range(2):
-            for c in range(NC // LANES):
-                rows = pl.ds((f * 2 + half) * NC + c * LANES, LANES)
-                block = sum(field[rows, :] for field in fields)
-                turned = block.T.reshape(LEV, 8, LANES)
-                cols = slice(c * LANES, (c + 1) * LANES)
-                value = dense[:, f, half * 8 : half * 8 + 8, cols] + turned
-                out[:, f, half * 8 : half * 8 + 8, cols] = value
-                if half == 0:
-                    ups[:, f, :, cols] = cy[:, f, 0:8, cols] * value
-        return carry
-
-    lax.fori_loop(0, LF, turn, 0)
-    west(out, cx, sides)
-
-
-def last_kernel(a, cx, cy, ups, sides, out, below, side_in, rot, *sems):
-    halo = Halo(ups, sides, below, side_in, rot, sems)
-    barrier = pltpu.get_barrier_semaphore()
-    expected = halo.greet(barrier)
-    halo.zero()
-    pl.semaphore_wait(barrier, expected)
-    halo.start()
-    interior(a, cx, cy, out, 0, LEV)
-    halo.relay()
-    halo.wait_rows()
-    patch_rows(out, below, side_in)
-    halo.wait_rotated()
-    patch_rotated(out, rot)
-    halo.finish()
+    halo2.finish()
+    packets(pl.ds(1, BANDS - 1), 0, b).wait_send()
+
+
+PARTS = 4
+
+
+def last_kernel(a, cx, cy, below, side_in, rot, out_hbm, out, sems):
+    step = LEV // PARTS
+    copies = []
+    for p in range(PARTS):
+        lo, hi = p * step, (p + 1) * step
+        interior(a, cx, cy, out, lo, hi)
+        patch_rows(out, below, side_in, lo, hi)
+        patch_rotated(out, rot, lo, hi)
+        copies.append(pltpu.make_async_copy(out.at[lo:hi], out_hbm.at[lo:hi], sems.at[p]))
+        copies[-1].start()
+    for copy in copies:
+        copy.wait()
 
 
 def params(mib, cid=None):
@@ -509,11 +544,12 @@
     vmem, anywhere = pl.BlockSpec(memory_space=pltpu.VMEM), pl.BlockSpec(memory_space=pl.ANY)
     field = jax.ShapeDtypeStruct(FIELD, F32)
     dma = pltpu.SemaphoreType.DMA
-    dense, recv, held_x, held_y = pl.pallas_call(
+    size = LEV * LF * RD
+    mid, held_x, held_y, below, side_in, rot = pl.pallas_call(
         first_kernel,
-        out_shape=(field, jax.ShapeDtypeStruct((BANDS, PACK, LANES), F32), field, field),
-        in_specs=[pl.BlockSpec(memory_space=pltpu.HBM)] * 7,
-        out_specs=(vmem, anywhere, vmem, vmem),
+        out_shape=[field] * 3 + [jax.ShapeDtypeStruct(shape, F32) for shape in landing()],
+        in_specs=[anywhere] * 7,
+        out_specs=[vmem] * 6,
         scratch_shapes=[
             pltpu.VMEM(FIELD, F32),
             pltpu.VMEM((1, BANDS, RAYS, LEV * K), BF16),
@@ -521,12 +557,14 @@
             pltpu.VMEM((1, 1, BANDS), I32),
             pltpu.VMEM((1, K, BANDS), I32),
             pltpu.VMEM((BANDS, PACK, LANES), F32),
-            dma((7,)), dma, dma, dma,
-            pltpu.VMEM(UPS, F32),
-            pltpu.VMEM(SIDES, F32),
-        ] + halo_in(),
-        compiler_params=params(28, 0),
-        name="sums_and_first_step",
+            pltpu.VMEM((BANDS, PACK, LANES), F32),
+            pltpu.VMEM((2 * size, DEPTH), BF16),
+            pltpu.VMEM((DEPTH, NC), BF16),
+            pltpu.VMEM((2 * LF * LEV, DEPTH), BF16),
+            dma((7,)), dma, dma((2,)), dma,
+        ] + [pltpu.VMEM(shape, F32) for shape in landing()] + halo_scratch() + halo_scratch(),
+        compiler_params=params(40, 0),
+        name="sums_and_adjoint",
     )(*(
         pltpu.with_memory_space_constraint(value, pltpu.HBM)
         for value in (
@@ -534,28 +572,15 @@
             jnp.swapaxes(ray_innov, 1, 2), jnp.swapaxes(ray_dest, 1, 2), jnp.swapaxes(ray_cols, 1, 2),
         )
     ))
-    mid, ups, sides = pl.pallas_call(
-        scatter_kernel,
-        out_shape=(field, jax.ShapeDtypeStruct(UPS, F32), jax.ShapeDtypeStruct(SIDES, F32)),
-        in_specs=[vmem] * 4,
-        out_specs=(vmem, vmem, vmem),
-        scratch_shapes=[
-            pltpu.VMEM((BANDS, LANES), I32),
-            pltpu.SMEM((BANDS, LANES), I32),
-            pltpu.VMEM((BANDS, CAP * 4, 8 * LANES), F32),
-        ] + [pltpu.VMEM((LF * 2 * NC, LANES), F32)] * COPIES + [dma],
-        compiler_params=params(36),
-        name="forcing",
-    )(recv, dense, held_x, held_y)
     return pl.pallas_call(
         last_kernel,
         out_shape=field,
-        in_specs=[vmem] * 5,
-        out_specs=vmem,
-        scratch_shapes=halo_in(),
-        compiler_params=params(28, 1),
+        in_specs=[vmem] * 6,
+        out_specs=anywhere,
+        scratch_shapes=[pltpu.VMEM(FIELD, F32), dma((PARTS,))],
+        compiler_params=params(24),
         name="second_step",
-    )(mid, held_x, held_y, ups, sides)
+    )(mid, held_x, held_y, below, side_in, rot)
 
 
 def solution(mesh):

time: 41.5 us -> 47.9 us (1.15)
  the two profiles are of different devices: /device:TPU:27 before, /device:TPU:1 now
where the time goes in v3:
time: 47.9 us; the launch traced here: 47.8 us
  Pallas kernels  47.8 us (100%)
    pallas_call x1, Pallas kernels, per_device(): pl.pallas_call(first_kernel, out_shape=[field] * 3 + [jax.ShapeDtypeStruc...  44 us
    pallas_call x1, Pallas kernels, per_device(): pl.pallas_call(last_kernel, out_shape=field, in_specs=[vmem] * 6, out_spe...  3.73 us

profile of v3, /device:TPU:1, one launch (start us, length us, event | category | flops | bytes accessed | tf_op | source)
XLA Modules:
  0.0 47.8 jit_solution(3157929816624657698)
XLA Ops:
  0.0 44.0 %sums_and_adjoint.1 = (f32[16,3,16,1024]{3,2,1,0:T(8,128)S(1)}, f32[16,3,16,1024]{3,2,1,0:T(8,128)S(1)}, f32[16,3,16,1024]{3,2,1,0:T(8,128)S(1)}, f32[16,3,1,102...) custom-call(f32[16,3,16,1024]{3,2,1,0:T(8,128)} %a_hbm.1, f32[16,3,16,1024]{3,2,1,0:T(8,128)} %cx_hbm.1, ...), custom_call_target="tpu_custom_call" | custom-call | tf_op jit(solution)/shard_map/sums_and_adjoint/pallas_call | solution.py:548
  44.0 3.7 %second_step.1 = f32[16,3,16,1024]{3,2,1,0:T(8,128)} custom-call(f32[16,3,16,1024]{3,2,1,0:T(8,128)S(1)} %get-tuple-element.11.a, f32[16,3,16,1024]{3,2,1,0:T(8,128)S(1)} %get-tuple-element.12.cx, f32[16,3,16,1024]{3,2,1,0:T(8,128)S(1)} %get-tuple-element.13.cy, f32[16,3,1,1024]{3,2,1,0:T(1,128)S(1)} %get-tuple-element.14.below, ...), custom_call_target="tpu_custom_call" | custom-call | tf_op jit(solution)/shard_map/second_step/pallas_call | solution.py:575

commit v4 on v3

--- a/solution.py
+++ b/solution.py
@@ -123,7 +123,7 @@
             self.rot_send.at[which, r], self.rot_recv.at[which], face, n,
         )
 
-    def start(self):
+    def start_rotated(self):
         g, b = self.g, self.b
 
         @pl.when(b == 0)
@@ -137,7 +137,6 @@
                     self.piece(0, 1, r, r * GROUP).start()
                 for r in range(1, RELAYS):
                     self.piece(1, 0, r, r * GROUP).start()
-                self.one(1, 2, 0, 0).start()
                 self.rot[1] = self.seam[1, :, NC - LANES :]
 
             @pl.when(g == 1)
@@ -146,6 +145,18 @@
                     self.seam[0, l : l + 1, :] = self.ups[l, 1, 0:1, :]
                 for r in range(RELAYS):
                     self.piece(0, 0, r, r * GROUP).start()
+
+    def start_rows(self):
+        g, b = self.g, self.b
+
+        @pl.when(b == 0)
+        def _():
+            @pl.when(g == 0)
+            def _():
+                self.one(1, 2, 0, 0).start()
+
+            @pl.when(g == 1)
+            def _():
                 self.one(0, 1, 1, 0).start()
                 self.one(2, 0, 0, 2).start()
 
@@ -296,13 +307,16 @@
     lax.fori_loop(lo, hi, body, 0)
 
 
-def patch_rows(out, below, side_in, lo, hi):
+def patch_rows(out, below, lo, hi):
     def body(l, carry):
         for f in range(LF):
             out[l, f, RD - 1 : RD, :] += below[l, f]
         return carry
 
     lax.fori_loop(lo, hi, body, 0)
+
+
+def patch_west(out, side_in, lo, hi):
     full = (hi - lo, RD, LANES)
     lane = iota(full, 2)
     mine = jnp.where(lane == iota(full, 0) + lo, jnp.broadcast_to(side_in[...][None], full), 0.0)
@@ -374,16 +388,15 @@
 
 HALF = BANDS // 2
 DEPTH = HALF * CAP * K
-WIDE = 256
-
-
-def one_hots(recv, first, left, right, top):
+COPIES = 4
+
+
+def factors(recv, first, right, top, spot, plain):
     flat = recv.reshape(BANDS * PACK, LANES)
     at = first * PACK
     codes = flat[pl.ds(at + SENT - 1, HALF, stride=PACK), :]
-    face_row = iota((LF * RD, LANES), 0)
     column = iota((LANES, NC), 1)
-    size = LEV * LF * RD
+    spot_row = iota((RD, LANES), 0)
     for pair in range(2):
         spots = [(s, 2 * pair + half) for half in range(2) for s in range(CAP)]
         sums = jnp.concatenate(
@@ -392,39 +405,27 @@
         cells = jnp.concatenate(
             [pltpu.roll(codes, (LANES - s * K - q * 8) % LANES, 1) for s, q in spots], axis=0
         )
-        rows = lax.shift_right_logical(cells.T.astype(I32), 10)
+        turned = cells.T.astype(I32)
+        rows = lax.shift_right_logical(turned, 10)
+        edge = jnp.where((turned & (NC - 1)) == 0, rows, LF * RD)
         cols = cells.astype(I32) & (NC - 1)
         for inner in range(8):
             part = slice((pair * 8 + inner) * LANES, (pair * 8 + inner + 1) * LANES)
             high, mid, _ = split(sums[inner * LEV : (inner + 1) * LEV])
             row = rows[inner : inner + 1]
-            chosen = jnp.where(face_row == row, 1.0, 0.0).astype(BF16)
             for n, term in enumerate((high, mid)):
-                product = term[:, None, :] * chosen[None]
-                left[n * size : (n + 1) * size, part] = product.reshape(size, LANES)
-                if top is not None:
-                    for f in range(LF):
-                        kept = jnp.where(row == f * RD, term.astype(F32), 0.0).astype(BF16)
-                        top[(n * LF + f) * LEV : (n * LF + f + 1) * LEV, part] = kept
+                plain[n * LEV : (n + 1) * LEV, part] = term
+                for f in range(LF):
+                    kept = jnp.where(row == f * RD, term.astype(F32), 0.0).astype(BF16)
+                    top[(n * LF + f) * LEV : (n * LF + f + 1) * LEV, part] = kept
+            spot[:, part] = jnp.where(spot_row == edge[inner : inner + 1], 1.0, 0.0).astype(BF16)
             right[part, :] = jnp.where(column == cols[:, inner : inner + 1], 1.0, 0.0).astype(BF16)
-
-
-def add_product(left, right, out, lo, hi):
-    size = LEV * LF * RD
-
-    def body(n, carry):
-        cols = pl.ds(pl.multiple_of(n * WIDE, WIDE), WIDE)
-        both = dot(left[...], right[:, cols])
-        out[:, :, :, cols] += (both[:size] + both[size:]).reshape(LEV, LF, RD, WIDE)
-        return carry
-
-    lax.fori_loop(lo, hi, body, 0)
 
 
 def first_kernel(
     a_hbm, cx_hbm, cy_hbm, tiles_hbm, innov_hbm, dest_hbm, cells_hbm,
-    out, cx, cy, below2, side_in2, rot2,
-    a, tiles, innov, dest, cells, send, recv, left, right, top, load_sem, pack_send, pack_recv, own_sem,
+    out, cx, cy, values, index, below2, side_in2, rot2,
+    a, tiles, innov, dest, cells, send, recv, right, top, spot, plain, sides_x, load_sem, pack_send, pack_recv, own_sem,
     below, side_in, rot, ups, sides, seam, sem1, sem2, sem3, sem4, sem5,
     ups2, sides2, seam2, *sems2,
 ):
@@ -454,18 +455,6 @@
     pack(tiles, innov, dest, cells, send)
     own = pltpu.make_async_copy(send.at[0, pl.ds(0, SENT)], recv.at[0, pl.ds(0, SENT)], own_sem)
     own.start()
-    for load in loads[4:]:
-        load.wait()
-
-    def lift(l, carry):
-        ups[l] = cy[l, :, 0:8, :] * a[l, :, 0:8, :]
-        return carry
-
-    lax.fori_loop(0, LEV, lift, 0)
-    west(cx[:, 0, :, 0:LANES] * a[:, 0, :, 0:LANES], sides)
-    pl.semaphore_wait(barrier, expected)
-    halo.start()
-    halo.side().start()
 
     def packets(which, half, band):
         return pltpu.make_async_remote_copy(
@@ -477,6 +466,18 @@
             device_id_type=MESH,
         )
 
+    for load in loads[4:]:
+        load.wait()
+
+    def lift(l, carry):
+        ups[l] = cy[l, :, 0:8, :] * a[l, :, 0:8, :]
+        return carry
+
+    lax.fori_loop(0, LEV, lift, 0)
+    west(cx[:, 0, :, 0:LANES] * a[:, 0, :, 0:LANES], sides)
+    pl.semaphore_wait(barrier, expected)
+    halo.start_rotated()
+    halo.side().start()
     for half in range(2):
 
         def ship(i, carry, half=half):
@@ -484,32 +485,38 @@
             return carry
 
         lax.fori_loop(max(1, half * HALF), (half + 1) * HALF, ship, 0)
+    halo.start_rows()
     halo.relay()
     interior(a, cx, cy, out, 0, LEV)
     own.wait()
-    packets(pl.ds(1, HALF - 1), 0, b).wait_recv()
-    one_hots(recv, 0, left, right, None)
-    add_product(left, right, out, 0, NC // WIDE)
-    halo.wait_rows()
+    edge_row = jnp.zeros((2 * LF * LEV, NC), F32)
+    edge_column = jnp.zeros((RD, LEV), F32)
+    for half in range(2):
+        low = max(1, half * HALF)
+        packets(pl.ds(low, (half + 1) * HALF - low), half, b).wait_recv()
+        factors(recv, half * HALF, right, top, spot, plain)
+        edge_row += dot(top[...], right[...])
+        edge_column += dot_t(spot[...], plain[0:LEV]) + dot_t(spot[...], plain[LEV:])
     halo.side().wait_recv()
-    patch_rows(out, below, side_in, 0, LEV)
     halo.wait_rotated()
     patch_rotated(out, rot, 0, LEV)
-    packets(pl.ds(HALF, HALF), 1, b).wait_recv()
-    one_hots(recv, HALF, left, right, top)
-    first = dot(top[...], right[...])
-    first = first[: LF * LEV] + first[LF * LEV :]
+    patch_west(out, side_in, 0, LEV)
+    edge_row = edge_row[: LF * LEV] + edge_row[LF * LEV :]
     for l in range(LEV):
         for f in range(LF):
-            value = out[l, f, 0:1, :] + first[f * LEV + l : f * LEV + l + 1]
+            value = out[l, f, 0:1, :] + edge_row[f * LEV + l : f * LEV + l + 1]
             ups2[l, f, 0:1, :] = cy[l, f, 0:1, :] * value
-    halo2.start()
-    add_product(left, right, out, 0, 1)
-    west(cx[:, 0, :, 0:LANES] * out[:, 0, :, 0:LANES], sides2)
+    halo2.start_rotated()
+    halo.wait_rows()
+    patch_rows(out, below, 0, LEV)
+    edge_column = jnp.concatenate([edge_column, jnp.zeros((RD, LANES - LEV), F32)], axis=1)
+    west(out[:, 0, :, 0:LANES], sides2)
+    west(cx[:, 0, :, 0:LANES], sides_x)
+    sides2[...] = (sides2[...] + edge_column) * sides_x[...]
     halo2.side().start()
-    add_product(left, right, out, 1, 2)
+    halo2.start_rows()
+    widen_rows(recv, values, index)
     halo2.relay()
-    add_product(left, right, out, 2, NC // WIDE)
     halo2.wait_rows()
     halo2.side().wait_recv()
     halo2.wait_rotated()
@@ -518,16 +525,68 @@
     packets(pl.ds(1, BANDS - 1), 0, b).wait_send()
 
 
+def widen_rows(recv, values, index):
+    shift = lax.shift_right_logical
+    from_lane, to_lane = iota((2 * LANES, 8 * LANES), 0) & (LANES - 1), iota((2 * LANES, 8 * LANES), 1)
+    widen = (shift(from_lane, 4) == shift(to_lane, 7)) & (
+        (from_lane & (LEV - 1)) == shift(to_lane & (LANES - 1), 3)
+    )
+    widen = jnp.where(widen, 1.0, 0.0).astype(BF16)
+    high, mid, _ = split(recv[:, 0 : CAP * 4, :].reshape(BANDS * CAP * 4, LANES))
+    wide = dot(jnp.concatenate([high, mid], axis=1), widen)
+    values[...] = wide.reshape(BANDS, CAP * 4, 8 * LANES)
+    flat = recv.reshape(BANDS * PACK, LANES)
+    cell = flat[pl.ds(SENT - 1, BANDS, stride=PACK), :].astype(I32)
+    index[...] = (shift(cell, 13) * NC + (cell & (NC - 1))) * 8 + (shift(cell, 10) & 7)
+
+
 PARTS = 4
 
 
-def last_kernel(a, cx, cy, below, side_in, rot, out_hbm, out, sems):
+def last_kernel(
+    values, index, dense, cx, cy, below, side_in, rot, out_hbm, index_s, mid, out, index_sem, sems, *fields
+):
+    to_scalar = pltpu.make_async_copy(index, index_s, index_sem)
+    to_scalar.start()
+
+    def clear(i, carry):
+        for field in fields:
+            field[pl.ds(i * LANES, LANES), :] = jnp.zeros((LANES, LANES), F32)
+        return carry
+
+    lax.fori_loop(0, LF * 2 * NC // LANES, clear, 0)
+    to_scalar.wait()
+    shift = lax.shift_right_logical
+    lane = iota((1, LANES), 1) & 7
+
+    def add(i, carry):
+        for e in range(CAP * K):
+            code = index_s[i, e]
+            line = values[i, e // 8 : e // 8 + 1, e % 8 * LANES : (e % 8 + 1) * LANES]
+            field = fields[e % COPIES]
+            field[pl.ds(shift(code, 3), 1), :] += jnp.where(lane == (code & 7), line, 0.0)
+        return carry
+
+    lax.fori_loop(0, BANDS, add, 0)
+
+    def turn(f, carry):
+        for half in range(2):
+            for c in range(NC // LANES):
+                rows = pl.ds((f * 2 + half) * NC + c * LANES, LANES)
+                block = sum(field[rows, :] for field in fields)
+                turned = block.T.reshape(LEV, 8, LANES)
+                cols = slice(c * LANES, (c + 1) * LANES)
+                mid[:, f, half * 8 : half * 8 + 8, cols] = dense[:, f, half * 8 : half * 8 + 8, cols] + turned
+        return carry
+
+    lax.fori_loop(0, LF, turn, 0)
     step = LEV // PARTS
     copies = []
     for p in range(PARTS):
         lo, hi = p * step, (p + 1) * step
-        interior(a, cx, cy, out, lo, hi)
-        patch_rows(out, below, side_in, lo, hi)
+        interior(mid, cx, cy, out, lo, hi)
+        patch_rows(out, below, lo, hi)
+        patch_west(out, side_in, lo, hi)
         patch_rotated(out, rot, lo, hi)
         copies.append(pltpu.make_async_copy(out.at[lo:hi], out_hbm.at[lo:hi], sems.at[p]))
         copies[-1].start()
@@ -544,12 +603,14 @@
     vmem, anywhere = pl.BlockSpec(memory_space=pltpu.VMEM), pl.BlockSpec(memory_space=pl.ANY)
     field = jax.ShapeDtypeStruct(FIELD, F32)
     dma = pltpu.SemaphoreType.DMA
-    size = LEV * LF * RD
-    mid, held_x, held_y, below, side_in, rot = pl.pallas_call(
+    dense, held_x, held_y, values, index, below, side_in, rot = pl.pallas_call(
         first_kernel,
-        out_shape=[field] * 3 + [jax.ShapeDtypeStruct(shape, F32) for shape in landing()],
+        out_shape=[field] * 3 + [
+            jax.ShapeDtypeStruct((BANDS, CAP * 4, 8 * LANES), F32),
+            jax.ShapeDtypeStruct((BANDS, LANES), I32),
+        ] + [jax.ShapeDtypeStruct(shape, F32) for shape in landing()],
         in_specs=[anywhere] * 7,
-        out_specs=[vmem] * 6,
+        out_specs=[vmem] * 8,
         scratch_shapes=[
             pltpu.VMEM(FIELD, F32),
             pltpu.VMEM((1, BANDS, RAYS, LEV * K), BF16),
@@ -558,13 +619,15 @@
             pltpu.VMEM((1, K, BANDS), I32),
             pltpu.VMEM((BANDS, PACK, LANES), F32),
             pltpu.VMEM((BANDS, PACK, LANES), F32),
-            pltpu.VMEM((2 * size, DEPTH), BF16),
             pltpu.VMEM((DEPTH, NC), BF16),
             pltpu.VMEM((2 * LF * LEV, DEPTH), BF16),
+            pltpu.VMEM((RD, DEPTH), BF16),
+            pltpu.VMEM((2 * LEV, DEPTH), BF16),
+            pltpu.VMEM(SIDES, F32),
             dma((7,)), dma, dma((2,)), dma,
         ] + [pltpu.VMEM(shape, F32) for shape in landing()] + halo_scratch() + halo_scratch(),
-        compiler_params=params(40, 0),
-        name="sums_and_adjoint",
+        compiler_params=params(28, 0),
+        name="sums_and_edges",
     )(*(
         pltpu.with_memory_space_constraint(value, pltpu.HBM)
         for value in (
@@ -575,12 +638,17 @@
     return pl.pallas_call(
         last_kernel,
         out_shape=field,
-        in_specs=[vmem] * 6,
+        in_specs=[vmem] * 8,
         out_specs=anywhere,
-        scratch_shapes=[pltpu.VMEM(FIELD, F32), dma((PARTS,))],
-        compiler_params=params(24),
-        name="second_step",
-    )(mid, held_x, held_y, below, side_in, rot)
+        scratch_shapes=[
+            pltpu.SMEM((BANDS, LANES), I32),
+            pltpu.VMEM(FIELD, F32),
+            pltpu.VMEM(FIELD, F32),
+            dma, dma((PARTS,)),
+        ] + [pltpu.VMEM((LF * 2 * NC, LANES), F32)] * COPIES,
+        compiler_params=params(28),
+        name="forcing_and_step",
+    )(values, index, dense, held_x, held_y, below, side_in, rot)
 
 
 def solution(mesh):

time: 47.9 us -> 39.4 us (0.82)
  the two profiles are of different devices: /device:TPU:1 before, /device:TPU:27 now
where the time goes in v4:
time: 39.4 us; the launch traced here: 39.3 us
  Pallas kernels  39.2 us (99%)
    pallas_call x1, Pallas kernels, per_device(): pl.pallas_call(first_kernel, out_shape=[field] * 3 + [jax.ShapeDtypeStruc...  26.4 us
    pallas_call x1, Pallas kernels, per_device(): pl.pallas_call(last_kernel, out_shape=field, in_specs=[vmem] * 8, out_spe...  12.8 us

profile of v4, /device:TPU:27, one launch (start us, length us, event | category | flops | bytes accessed | tf_op | source)
XLA Modules:
  0.0 39.3 jit_solution(13495408735160170595)
XLA Ops:
  0.0 26.4 %sums_and_edges.1 = (f32[16,3,16,1024]{3,2,1,0:T(8,128)S(1)}, f32[16,3,16,1024]{3,2,1,0:T(8,128)S(1)}, f32[16,3,16,1024]{3,2,1,0:T(8,128)S(1)}, f32[64,8,1024]{2...) custom-call(f32[16,3,16,1024]{3,2,1,0:T(8,128)} %a_hbm.1, ...), custom_call_target="tpu_custom_call" | custom-call | tf_op jit(solution)/shard_map/sums_and_edges/pallas_call | solution.py:606
  26.5 12.8 %forcing_and_step.1 = f32[16,3,16,1024]{3,2,1,0:T(8,128)} custom-call(f32[64,8,1024]{2,1,0:T(8,128)S(1)} %get-tuple-element.13.values, s32[64,128]{1,0:T(8,128)S(1)} %get-tuple-element.14.index, f32[16,3,16,1024]{3,2,1,0:T(8,128)S(1)} %get-tuple-element.15.dense, f32[16,3,16,1024]{3,2,1,0:T(8,128)S(1)} %get-tuple-element.16.cx, ...), custom_call_target="tpu_custom_call" | custom-call | tf_op jit(solution)/shard_map/forcing_and_step/pallas_call | solution.py:638

commit v5 on v4

--- a/solution.py
+++ b/solution.py
@@ -388,7 +388,7 @@
 
 HALF = BANDS // 2
 DEPTH = HALF * CAP * K
-COPIES = 4
+COPIES = 6
 
 
 def factors(recv, first, right, top, spot, plain):
@@ -527,17 +527,23 @@
 
 def widen_rows(recv, values, index):
     shift = lax.shift_right_logical
-    from_lane, to_lane = iota((2 * LANES, 8 * LANES), 0) & (LANES - 1), iota((2 * LANES, 8 * LANES), 1)
-    widen = (shift(from_lane, 4) == shift(to_lane, 7)) & (
-        (from_lane & (LEV - 1)) == shift(to_lane & (LANES - 1), 3)
-    )
+    wide = (2 * LANES, 8 * LANES)
+    from_lane, to_lane = iota(wide, 0) & (LANES - 1), iota(wide, 1)
+    block, inner = shift(to_lane, 7), to_lane & (LANES - 1)
+    widen = (shift(from_lane, 4) == block) & ((from_lane & (LEV - 1)) == shift(inner, 3))
     widen = jnp.where(widen, 1.0, 0.0).astype(BF16)
-    high, mid, _ = split(recv[:, 0 : CAP * 4, :].reshape(BANDS * CAP * 4, LANES))
-    wide = dot(jnp.concatenate([high, mid], axis=1), widen)
-    values[...] = wide.reshape(BANDS, CAP * 4, 8 * LANES)
     flat = recv.reshape(BANDS * PACK, LANES)
     cell = flat[pl.ds(SENT - 1, BANDS, stride=PACK), :].astype(I32)
-    index[...] = (shift(cell, 13) * NC + (cell & (NC - 1))) * 8 + (shift(cell, 10) & 7)
+    index[...] = shift(cell, 13) * NC + (cell & (NC - 1))
+    lower = (shift(cell, 10) & 7).astype(F32).astype(BF16)
+    own = (iota((BANDS, 8 * LANES), 1) & 7).astype(F32)
+    for s in range(CAP * 4):
+        high, mid, _ = split(flat[pl.ds(s, BANDS, stride=PACK), :])
+        lines = dot(jnp.concatenate([high, mid], axis=1), widen)
+        spread = jnp.where(from_lane[:LANES] == s * 8 + block[:LANES], 1.0, 0.0).astype(BF16)
+        lines = jnp.where(dot(lower, spread) == own, lines, 0.0)
+        for p in range(8):
+            values[s * 8 + p] = lines[:, p * LANES : (p + 1) * LANES]
 
 
 PARTS = 4
@@ -556,18 +562,13 @@
 
     lax.fori_loop(0, LF * 2 * NC // LANES, clear, 0)
     to_scalar.wait()
-    shift = lax.shift_right_logical
-    lane = iota((1, LANES), 1) & 7
-
     def add(i, carry):
-        for e in range(CAP * K):
-            code = index_s[i, e]
-            line = values[i, e // 8 : e // 8 + 1, e % 8 * LANES : (e % 8 + 1) * LANES]
+        for e in range(BANDS):
             field = fields[e % COPIES]
-            field[pl.ds(shift(code, 3), 1), :] += jnp.where(lane == (code & 7), line, 0.0)
+            field[pl.ds(index_s[e, i], 1), :] += values[i, e : e + 1, :]
         return carry
 
-    lax.fori_loop(0, BANDS, add, 0)
+    lax.fori_loop(0, CAP * K, add, 0)
 
     def turn(f, carry):
         for half in range(2):
@@ -606,7 +607,7 @@
     dense, held_x, held_y, values, index, below, side_in, rot = pl.pallas_call(
         first_kernel,
         out_shape=[field] * 3 + [
-            jax.ShapeDtypeStruct((BANDS, CAP * 4, 8 * LANES), F32),
+            jax.ShapeDtypeStruct((CAP * K, BANDS, LANES), F32),
             jax.ShapeDtypeStruct((BANDS, LANES), I32),
         ] + [jax.ShapeDtypeStruct(shape, F32) for shape in landing()],
         in_specs=[anywhere] * 7,
@@ -646,7 +647,7 @@
             pltpu.VMEM(FIELD, F32),
             dma, dma((PARTS,)),
         ] + [pltpu.VMEM((LF * 2 * NC, LANES), F32)] * COPIES,
-        compiler_params=params(28),
+        compiler_params=params(34),
         name="forcing_and_step",
     )(values, index, dense, held_x, held_y, below, side_in, rot)
 

time: 39.4 us -> 38.3 us (0.972)
  Pallas kernels: 39.2 us -> 38.2 us
    pallas_call x1, Pallas kernels: 12.8 us -> 11.7 us  [per_device(): pl.pallas_call(last_kernel, out_shape=field, in_specs=[vmem] * 8, out_spe...]
where the time goes in v5:
time: 38.3 us; the launch traced here: 38.2 us
  Pallas kernels  38.2 us (100%)
    pallas_call x1, Pallas kernels, per_device(): pl.pallas_call(first_kernel, out_shape=[field] * 3 + [jax.ShapeDtypeStruc...  26.4 us
    pallas_call x1, Pallas kernels, per_device(): pl.pallas_call(last_kernel, out_shape=field, in_specs=[vmem] * 8, out_spe...  11.7 us

profile of v5, /device:TPU:27, one launch (start us, length us, event | category | flops | bytes accessed | tf_op | source)
XLA Modules:
  0.0 38.2 jit_solution(4881036366201986730)
XLA Ops:
  0.0 26.4 %sums_and_edges.1 = (f32[16,3,16,1024]{3,2,1,0:T(8,128)S(1)}, f32[16,3,16,1024]{3,2,1,0:T(8,128)S(1)}, f32[16,3,16,1024]{3,2,1,0:T(8,128)S(1)}, f32[64,64,128]{2...) custom-call(f32[16,3,16,1024]{3,2,1,0:T(8,128)} %a_hbm.1, ...), custom_call_target="tpu_custom_call" | custom-call | tf_op jit(solution)/shard_map/sums_and_edges/pallas_call | solution.py:607
  26.5 11.7 %forcing_and_step.1 = f32[16,3,16,1024]{3,2,1,0:T(8,128)} custom-call(f32[64,64,128]{2,1,0:T(8,128)S(1)} %get-tuple-element.13.values, s32[64,128]{1,0:T(8,128)S(1)} %get-tuple-element.14.index, f32[16,3,16,1024]{3,2,1,0:T(8,128)S(1)} %get-tuple-element.15.dense, f32[16,3,16,1024]{3,2,1,0:T(8,128)S(1)} %get-tuple-element.16.cx, ...), custom_call_target="tpu_custom_call" | custom-call | tf_op jit(solution)/shard_map/forcing_and_step/pallas_call | solution.py:639

commit v6 on v5

--- a/solution.py
+++ b/solution.py
@@ -478,7 +478,7 @@
     pl.semaphore_wait(barrier, expected)
     halo.start_rotated()
     halo.side().start()
-    for half in range(2):
+    for half in (1, 0):
 
         def ship(i, carry, half=half):
             packets(i, half, (b + i) & (BANDS - 1)).start()
@@ -491,7 +491,7 @@
     own.wait()
     edge_row = jnp.zeros((2 * LF * LEV, NC), F32)
     edge_column = jnp.zeros((RD, LEV), F32)
-    for half in range(2):
+    for half in (1, 0):
         low = max(1, half * HALF)
         packets(pl.ds(low, (half + 1) * HALF - low), half, b).wait_recv()
         factors(recv, half * HALF, right, top, spot, plain)

time: 38.3 us -> 38 us (level)
  no operation moved by 1% of the time
where the time goes in v6:
time: 38 us
  Pallas kernels  37.9 us (100%)
    pallas_call x1, Pallas kernels, per_device(): pl.pallas_call(first_kernel, out_shape=[field] * 3 + [jax.ShapeDtypeStruc...  26.2 us
    pallas_call x1, Pallas kernels, per_device(): pl.pallas_call(last_kernel, out_shape=field, in_specs=[vmem] * 8, out_spe...  11.7 us

profile of v6, /device:TPU:27, one launch (start us, length us, event | category | flops | bytes accessed | tf_op | source)
XLA Modules:
  0.0 38.0 jit_solution(8521934514713919339)
XLA Ops:
  0.0 26.2 %sums_and_edges.1 = (f32[16,3,16,1024]{3,2,1,0:T(8,128)S(1)}, f32[16,3,16,1024]{3,2,1,0:T(8,128)S(1)}, f32[16,3,16,1024]{3,2,1,0:T(8,128)S(1)}, f32[64,64,128]{2...) custom-call(f32[16,3,16,1024]{3,2,1,0:T(8,128)} %a_hbm.1, ...), custom_call_target="tpu_custom_call" | custom-call | tf_op jit(solution)/shard_map/sums_and_edges/pallas_call | solution.py:607
  26.2 11.7 %forcing_and_step.1 = f32[16,3,16,1024]{3,2,1,0:T(8,128)} custom-call(f32[64,64,128]{2,1,0:T(8,128)S(1)} %get-tuple-element.13.values, s32[64,128]{1,0:T(8,128)S(1)} %get-tuple-element.14.index, f32[16,3,16,1024]{3,2,1,0:T(8,128)S(1)} %get-tuple-element.15.dense, f32[16,3,16,1024]{3,2,1,0:T(8,128)S(1)} %get-tuple-element.16.cx, ...), custom_call_target="tpu_custom_call" | custom-call | tf_op jit(solution)/shard_map/forcing_and_step/pallas_call | solution.py:639
